TPU v7x, 256 devices: a whole 4x4x8 slice. The times are simulated.
256 devices in a mesh: dp: 64 (over z, x_hi, y), mp: 4 (over x_lo, core).
Axes of the slice: x: 4 (x_hi: 2, x_lo: 2; x = x_hi * 2 + x_lo), y: 4, z: 8, core: 2. Of those that a mesh axis runs over, the one named last changes fastest.
Arguments:
- images: bfloat16 [8192, 1152], P('dp'), may hold values from -16 to 16
- captions: bfloat16 [8192, 1152], P('dp'), may hold values from -16 to 16
- image_gain: float32 [1152], replicated, may hold values from 0.5 to 1.5
- fc_in: bfloat16 [1152, 4304], P(None, 'mp'), may hold values from -0.1875 to 0.1875
- fc_out: bfloat16 [4304, 1152], P('mp'), may hold values from -0.09375 to 0.09375
- text_gain: float32 [1152], replicated, may hold values from 0.5 to 1.5
- text_head: bfloat16 [1152, 1152], P(None, 'mp'), may hold values from -2 to 2
- caption_ids: int32 [64, 128], P('dp'), may hold values from 0 to 127, as said below
- logit_scale: float32 [1], replicated, may hold values from 20 to 40
- logit_bias: float32 [1], replicated, may hold values from -12 to -8
Outputs:
- row_loss: float32 [8192], P('dp')
- grad_in: float32 [1152, 4304], P('dp', 'mp')
- grad_out: float32 [4304, 1152], P('mp', 'dp')
- grad_head: float32 [1152, 1152], P('dp', 'mp')
Inputs may be any that keep to these rules, and one draw needn't show every extreme that they name: Each row of caption_ids is a permutation of the 128 caption rows of its index of dp.
All inputs are finite; a program needn't handle non-finite values.
Results may differ from a plain program's by a relative error of at most 0.003.
Values may be sent and summed in bfloat16 or wider, within the bound.
A program may use at most 128 MiB of HBM per device.

v0:
```python
import jax
import jax.numpy as jnp
from jax import lax
from jax.sharding import PartitionSpec as P


def shifted(shard, axis, by):
    length = lax.axis_size(axis)
    return lax.ppermute(shard, axis, [(i, (i + by) % length) for i in range(length)])


def layer_norm(values, gain):
    center = values - jnp.mean(values, -1, keepdims=True)
    spread = jnp.mean(center * center, -1, keepdims=True)
    return center * lax.rsqrt(spread + 1e-06) * gain


def unit_rows(values):
    return values * lax.rsqrt(jnp.sum(values * values, -1, keepdims=True) + 1e-06)


def inner_rows(left, right):
    return lax.dot_general(
        left, right, (((0,), (0,)), ((), ())), preferred_element_type=jnp.float32
    )


def signed_terms(left, right, sign, scale, bias):
    logit = (
        scale
        * lax.dot_general(left, right, (((1,), (1,)), ((), ())), preferred_element_type=jnp.float32)
        + bias
    )
    loss = jnp.sum(jax.nn.softplus(-sign * logit), 1)
    slope = (-sign * jax.nn.sigmoid(-sign * logit) * scale).astype(jnp.bfloat16)
    return (loss, slope)


def on_device(
    images,
    captions,
    image_gain,
    fc_in,
    fc_out,
    text_gain,
    text_head,
    caption_ids,
    logit_scale,
    logit_bias,
):
    inputs = images.astype(jnp.float32)
    normed = layer_norm(inputs, image_gain).astype(jnp.bfloat16)
    pre = jnp.dot(normed, fc_in, preferred_element_type=jnp.float32)
    act = jax.nn.gelu(pre).astype(jnp.bfloat16)
    partial_out = jnp.dot(act, fc_out, preferred_element_type=jnp.float32)
    feat = inputs + lax.psum(partial_out, "mp")
    img_home = unit_rows(feat).astype(jnp.bfloat16)
    text_normed = layer_norm(captions.astype(jnp.float32), text_gain).astype(jnp.bfloat16)
    head_part = jnp.dot(text_normed, text_head, preferred_element_type=jnp.float32).astype(
        jnp.bfloat16
    )
    head = lax.all_gather(head_part, "mp", axis=1, tiled=True)
    head_wide = head.astype(jnp.float32)
    txt_home = unit_rows(head_wide).astype(jnp.bfloat16)
    scale = logit_scale[0]
    bias = logit_bias[0]
    rows = img_home.shape[0]
    own = caption_ids[0][:, None] == jnp.arange(rows, dtype=jnp.int32)[None, :]
    sign_home = jnp.where(own, 1.0, -1.0).astype(jnp.float32)
    loss_home, slope_home = signed_terms(img_home, txt_home, sign_home, scale, bias)
    d_img_home = jnp.dot(slope_home, txt_home, preferred_element_type=jnp.float32)
    d_txt_home = inner_rows(slope_home, img_home)

    def visit(pair, sums):
        img_away, txt_away = pair
        loss_a, slope_a = signed_terms(img_home, txt_away, -1.0, scale, bias)
        loss_b, slope_b = signed_terms(img_away, txt_home, -1.0, scale, bias)
        return (
            sums[0] + loss_a,
            sums[1] + jnp.dot(slope_a, txt_away, preferred_element_type=jnp.float32),
            sums[2] + inner_rows(slope_b, img_away),
        )

    group = min(16, lax.axis_size("dp"))
    stride = lax.axis_size("dp") // group

    def circle_turn(count, carry):
        held, sums = carry
        held = shifted((held[0], held[1]), "dp", stride)
        return (held, visit(held, sums))

    held, totals = lax.fori_loop(
        0, group - 1, circle_turn, ((img_home, txt_home), (loss_home, d_img_home, d_txt_home))
    )
    row_loss, d_img, d_txt = totals
    d_feat = jax.vjp(unit_rows, feat)[1](d_img)[0].astype(jnp.bfloat16)
    d_act = lax.dot_general(
        d_feat, fc_out, (((1,), (1,)), ((), ())), preferred_element_type=jnp.float32
    )
    d_pre = jax.vjp(jax.nn.gelu, pre)[1](d_act)[0].astype(jnp.bfloat16)
    d_head = jax.vjp(unit_rows, head_wide)[1](d_txt)[0].astype(jnp.bfloat16)
    cols = head_part.shape[1]
    d_cols = lax.dynamic_slice_in_dim(d_head, lax.axis_index("mp") * cols, cols, 1)
    hidden = d_pre.shape[1]
    joined = lax.psum_scatter(
        jnp.concatenate([inner_rows(normed, d_pre), inner_rows(text_normed, d_cols)], 1),
        "dp",
        scatter_dimension=0,
        tiled=True,
    )
    grad_in = joined[:, :hidden]
    grad_head = joined[:, hidden:]
    grad_out = lax.psum_scatter(inner_rows(act, d_feat), "dp", scatter_dimension=1, tiled=True)
    return (row_loss, grad_in, grad_out, grad_head)


def solution(mesh):
    placed = (
        P("dp", None),
        P("dp", None),
        P(),
        P(None, "mp"),
        P("mp", None),
        P(),
        P(None, "mp"),
        P("dp", None),
        P(),
        P(),
    )
    return jax.shard_map(
        on_device,
        mesh=mesh,
        in_specs=placed,
        out_specs=(P("dp"), P("dp", "mp"), P("mp", "dp"), P("dp", "mp")),
        check_vma=False,
    )
```

profile of v0, /device:TPU:32, one launch (start us, length us, event | category | flops | bytes accessed | tf_op | source)
XLA Modules:
  0.0 1167.0 jit_solution(13781159701319132493)
XLA Ops:
  9.7 2.8 fusion.62
  16.8 5.9 all_gather.3
  26.1 34.6 %all-reduce.6.cloned.1.call-done = f32[128,1152]{1,0:T(8,128)} async-done(((f32[128,1152]{1,0:T(8,128)}), f32[128,1152]{1,0:T(8,128)}) %all-reduce.6.cloned.1.call-update) | async-done | bytes 589840 | tf_op jit(solution)/shard_map/psum | solution.py:56
  65.5 328.3 %while.18 = (s32[]{:T(128)}, bf16[128,1152]{1,0:T(8,128)(2,1)}, bf16[128,1152]{1,0:T(8,128)(2,1)}, f32[128]{0:T(128)S(1)}, f32[128,1152]{1,0:T(8,128)S(1)}, /*in...) while((s32[]{:T(128)}, bf16[128,1152]{1,0:T(8,128)(2,1)}, ...), condition=%wide.region_10.11_spmd, body=%wide.region_8.10_spmd.sunk | while | flops 151633920 | bytes 7506129 | solution.py:92
  65.5 2.7 collective-permute-start.1
  70.1 8.0 collective-permute-done.1
  86.3 3.8 convolution_add_fusion.5
  91.9 2.7 collective-permute-start
  94.7 8.1 collective-permute-done.1
  102.8 2.6 fusion.97
  110.2 3.8 convolution_add_fusion.5
  114.9 3.6 collective-permute-start
  118.5 8.2 collective-permute-done.1
  126.6 2.6 fusion.97
  133.6 3.8 convolution_add_fusion.5
  137.4 4.5 collective-permute-start
  141.9 7.4 collective-permute-done.1
  149.4 2.6 fusion.97
  156.3 3.8 convolution_add_fusion.5
  160.2 4.5 collective-permute-start
  164.6 5.3 collective-permute-done.1
  170.0 2.6 fusion.97
  176.9 3.8 convolution_add_fusion.5
  180.9 4.3 collective-permute-start
  185.2 5.2 collective-permute-done.1
  190.5 2.6 fusion.97
  197.4 3.8 convolution_add_fusion.5
  201.3 4.2 collective-permute-start
  205.5 6.1 collective-permute-done.1
  211.6 2.6 fusion.97
  218.6 3.8 convolution_add_fusion.5
  222.4 3.9 collective-permute-start
  226.3 6.7 collective-permute-done.1
  233.0 2.6 fusion.97
  240.0 3.8 convolution_add_fusion.5
  243.8 2.7 collective-permute-start
  246.5 8.0 collective-permute-done.1
  254.5 2.6 fusion.97
  261.4 3.8 convolution_add_fusion.5
  266.7 9.2 collective-permute-done.1
  275.9 2.6 fusion.97
  282.9 3.8 convolution_add_fusion.5
  288.0 9.3 collective-permute-done.1
  297.3 2.6 fusion.97
  304.3 3.8 convolution_add_fusion.5
  308.1 3.8 collective-permute-start
  311.9 6.8 collective-permute-done.1
  318.8 2.6 fusion.97
  325.7 3.8 convolution_add_fusion.5
  329.6 5.5 collective-permute-start
  335.1 5.1 collective-permute-done.1
  340.2 2.6 fusion.97
  347.2 3.8 convolution_add_fusion.5
  353.1 5.1 collective-permute-start
  358.2 3.4 collective-permute-done.1
  361.6 2.6 fusion.97
  368.6 3.8 convolution_add_fusion.5
  372.4 4.4 collective-permute-start.1
  376.9 4.8 collective-permute-start
  390.0 3.8 convolution_add_fusion.5
  397.3 6.3 fusion.36
  403.6 4.4 fusion.64
  411.8 5.5 pad_maximum_fusion
  419.2 735.2 %all-reduce.8.cloned.1.call-done = (f32[1152,1364]{0,1:T(8,128)}, f32[1076,1152]{0,1:T(8,128)}) async-done(((f32[1152,1364]{0,1:T(8,128)}, f32[1076,1152]{0,1:T(8,128)}), (f32[1152,1364]{0,1:T(8,128)}, f32[1076,1152]{0,1:T(8,128)})) %all-reduce.8.cloned.1.call-update) | async-done | bytes 11243536
  (164 shorter events, 110.4 us)
Async XLA Ops:
  7.2 6.1 copy-start
  7.2 53.5 %all-reduce.6.cloned.1.call-start = ((), (), s32[]{:S(2)}) async-start(), calls=%async_computation | async-start | bytes 1179648 | tf_op jit(solution)/shard_map/psum | solution.py:56
  12.5 0.8 copy-start.5
  13.3 1.6 copy-start.8
  13.3 2.0 copy-start.11
  14.8 1139.6 %all-reduce.8.cloned.1.call-start = ((), (), s32[]{:S(2)}) async-start(), calls=%async_computation.1 | async-start | bytes 23224320
  15.0 45.7 %copy-start.2 = (bf16[128,1152]{1,0:T(8,128)(2,1)S(1)}, bf16[128,1152]{1,0:T(8,128)(2,1)}, u32[]{:S(2)}) copy-start(bf16[128,1152]{1,0:T(8,128)(2,1)} %param.12) | copy-start | bytes 884740
  22.7 1.0 copy-start.6
  22.9 40.9 %copy-start.12 = (s32[1,128]{1,0:T(1,128)S(1)}, s32[1,128]{1,0:T(1,128)}, u32[]{:S(2)}) copy-start(s32[1,128]{1,0:T(1,128)} %param.19) | copy-start | bytes 1540
  24.0 40.2 %copy-start.4 = (bf16[128,1152]{1,0:T(8,128)(2,1)}, bf16[128,1152]{1,0:T(8,128)(2,1)S(1)}, u32[]{:S(2)}) copy-start(bf16[128,1152]{1,0:T(8,128)(2,1)S(1)} %copy.20) | copy-start | bytes 884740
  63.1 2.5 copy-start.9
  65.5 12.5 %collective-permute-start.1 = (bf16[128,1152]{1,0:T(8,128)(2,1)}, bf16[128,1152]{1,0:T(8,128)(2,1)}, u32[]{:S(2)}, u32[]{:S(2)}) collective-permute-start(bf16[128,1152]{1,0:T(8,128)(2,1)} %get-tuple-element.193), channel_id=1, source_target_pairs={{0,16},{4,20},{8,24},{12,28},{16,32},{20,36},{24,40},{28,44},{32,4... | collective-permute-start | bytes 884744 | tf_op jit(solution)/shard_map/while/body/eval_jaxpr/ppermute | solution.py:9
  68.2 15.5 %collective-permute-start = (bf16[128,1152]{1,0:T(8,128)(2,1)}, bf16[128,1152]{1,0:T(8,128)(2,1)S(1)}, u32[]{:S(2)}, u32[]{:S(2)}) collective-permute-start(bf16[128,1152]{1,0:T(8,128)(2,1)} %get-tuple-element.192), channel_id=1, source_target_pairs={{0,16},{4,20},{8,24},{12,28},{16,32},{20,36},{24,40},{28,44},{32,4... | collective-permute-start | bytes 884744 | tf_op jit(solution)/shard_map/while/body/eval_jaxpr/ppermute | solution.py:9
  90.2 12.7 %collective-permute-start.1 = (bf16[128,1152]{1,0:T(8,128)(2,1)}, bf16[128,1152]{1,0:T(8,128)(2,1)}, u32[]{:S(2)}, u32[]{:S(2)}) collective-permute-start(bf16[128,1152]{1,0:T(8,128)(2,1)} %get-tuple-element.193), channel_id=1, source_target_pairs={{0,16},{4,20},{8,24},{12,28},{16,32},{20,36},{24,40},{28,44},{32,4... | collective-permute-start | bytes 884744 | tf_op jit(solution)/shard_map/while/body/eval_jaxpr/ppermute | solution.py:9
  91.9 15.6 %collective-permute-start = (bf16[128,1152]{1,0:T(8,128)(2,1)}, bf16[128,1152]{1,0:T(8,128)(2,1)S(1)}, u32[]{:S(2)}, u32[]{:S(2)}) collective-permute-start(bf16[128,1152]{1,0:T(8,128)(2,1)} %get-tuple-element.192), channel_id=1, source_target_pairs={{0,16},{4,20},{8,24},{12,28},{16,32},{20,36},{24,40},{28,44},{32,4... | collective-permute-start | bytes 884744 | tf_op jit(solution)/shard_map/while/body/eval_jaxpr/ppermute | solution.py:9
  114.0 12.7 %collective-permute-start.1 = (bf16[128,1152]{1,0:T(8,128)(2,1)}, bf16[128,1152]{1,0:T(8,128)(2,1)}, u32[]{:S(2)}, u32[]{:S(2)}) collective-permute-start(bf16[128,1152]{1,0:T(8,128)(2,1)} %get-tuple-element.193), channel_id=1, source_target_pairs={{0,16},{4,20},{8,24},{12,28},{16,32},{20,36},{24,40},{28,44},{32,4... | collective-permute-start | bytes 884744 | tf_op jit(solution)/shard_map/while/body/eval_jaxpr/ppermute | solution.py:9
  114.9 16.2 %collective-permute-start = (bf16[128,1152]{1,0:T(8,128)(2,1)}, bf16[128,1152]{1,0:T(8,128)(2,1)S(1)}, u32[]{:S(2)}, u32[]{:S(2)}) collective-permute-start(bf16[128,1152]{1,0:T(8,128)(2,1)} %get-tuple-element.192), channel_id=1, source_target_pairs={{0,16},{4,20},{8,24},{12,28},{16,32},{20,36},{24,40},{28,44},{32,4... | collective-permute-start | bytes 884744 | tf_op jit(solution)/shard_map/while/body/eval_jaxpr/ppermute | solution.py:9
  137.4 11.9 %collective-permute-start.1 = (bf16[128,1152]{1,0:T(8,128)(2,1)}, bf16[128,1152]{1,0:T(8,128)(2,1)}, u32[]{:S(2)}, u32[]{:S(2)}) collective-permute-start(bf16[128,1152]{1,0:T(8,128)(2,1)} %get-tuple-element.193), channel_id=1, source_target_pairs={{0,16},{4,20},{8,24},{12,28},{16,32},{20,36},{24,40},{28,44},{32,4... | collective-permute-start | bytes 884744 | tf_op jit(solution)/shard_map/while/body/eval_jaxpr/ppermute | solution.py:9
  137.4 16.3 %collective-permute-start = (bf16[128,1152]{1,0:T(8,128)(2,1)}, bf16[128,1152]{1,0:T(8,128)(2,1)S(1)}, u32[]{:S(2)}, u32[]{:S(2)}) collective-permute-start(bf16[128,1152]{1,0:T(8,128)(2,1)} %get-tuple-element.192), channel_id=1, source_target_pairs={{0,16},{4,20},{8,24},{12,28},{16,32},{20,36},{24,40},{28,44},{32,4... | collective-permute-start | bytes 884744 | tf_op jit(solution)/shard_map/while/body/eval_jaxpr/ppermute | solution.py:9
  160.2 9.8 collective-permute-start.1
  160.2 14.2 %collective-permute-start = (bf16[128,1152]{1,0:T(8,128)(2,1)}, bf16[128,1152]{1,0:T(8,128)(2,1)S(1)}, u32[]{:S(2)}, u32[]{:S(2)}) collective-permute-start(bf16[128,1152]{1,0:T(8,128)(2,1)} %get-tuple-element.192), channel_id=1, source_target_pairs={{0,16},{4,20},{8,24},{12,28},{16,32},{20,36},{24,40},{28,44},{32,4... | collective-permute-start | bytes 884744 | tf_op jit(solution)/shard_map/while/body/eval_jaxpr/ppermute | solution.py:9
  180.7 9.7 collective-permute-start.1
  180.9 13.9 %collective-permute-start = (bf16[128,1152]{1,0:T(8,128)(2,1)}, bf16[128,1152]{1,0:T(8,128)(2,1)S(1)}, u32[]{:S(2)}, u32[]{:S(2)}) collective-permute-start(bf16[128,1152]{1,0:T(8,128)(2,1)} %get-tuple-element.192), channel_id=1, source_target_pairs={{0,16},{4,20},{8,24},{12,28},{16,32},{20,36},{24,40},{28,44},{32,4... | collective-permute-start | bytes 884744 | tf_op jit(solution)/shard_map/while/body/eval_jaxpr/ppermute | solution.py:9
  201.2 10.4 collective-permute-start.1
  201.3 14.7 %collective-permute-start = (bf16[128,1152]{1,0:T(8,128)(2,1)}, bf16[128,1152]{1,0:T(8,128)(2,1)S(1)}, u32[]{:S(2)}, u32[]{:S(2)}) collective-permute-start(bf16[128,1152]{1,0:T(8,128)(2,1)} %get-tuple-element.192), channel_id=1, source_target_pairs={{0,16},{4,20},{8,24},{12,28},{16,32},{20,36},{24,40},{28,44},{32,4... | collective-permute-start | bytes 884744 | tf_op jit(solution)/shard_map/while/body/eval_jaxpr/ppermute | solution.py:9
  222.4 10.6 collective-permute-start.1
  222.4 15.0 %collective-permute-start = (bf16[128,1152]{1,0:T(8,128)(2,1)}, bf16[128,1152]{1,0:T(8,128)(2,1)S(1)}, u32[]{:S(2)}, u32[]{:S(2)}) collective-permute-start(bf16[128,1152]{1,0:T(8,128)(2,1)} %get-tuple-element.192), channel_id=1, source_target_pairs={{0,16},{4,20},{8,24},{12,28},{16,32},{20,36},{24,40},{28,44},{32,4... | collective-permute-start | bytes 884744 | tf_op jit(solution)/shard_map/while/body/eval_jaxpr/ppermute | solution.py:9
  243.8 10.7 collective-permute-start.1
  243.8 15.0 %collective-permute-start = (bf16[128,1152]{1,0:T(8,128)(2,1)}, bf16[128,1152]{1,0:T(8,128)(2,1)S(1)}, u32[]{:S(2)}, u32[]{:S(2)}) collective-permute-start(bf16[128,1152]{1,0:T(8,128)(2,1)} %get-tuple-element.192), channel_id=1, source_target_pairs={{0,16},{4,20},{8,24},{12,28},{16,32},{20,36},{24,40},{28,44},{32,4... | collective-permute-start | bytes 884744 | tf_op jit(solution)/shard_map/while/body/eval_jaxpr/ppermute | solution.py:9
  265.3 10.6 collective-permute-start.1
  265.3 15.0 %collective-permute-start = (bf16[128,1152]{1,0:T(8,128)(2,1)}, bf16[128,1152]{1,0:T(8,128)(2,1)S(1)}, u32[]{:S(2)}, u32[]{:S(2)}) collective-permute-start(bf16[128,1152]{1,0:T(8,128)(2,1)} %get-tuple-element.192), channel_id=1, source_target_pairs={{0,16},{4,20},{8,24},{12,28},{16,32},{20,36},{24,40},{28,44},{32,4... | collective-permute-start | bytes 884744 | tf_op jit(solution)/shard_map/while/body/eval_jaxpr/ppermute | solution.py:9
  286.7 10.7 collective-permute-start.1
  286.7 15.0 %collective-permute-start = (bf16[128,1152]{1,0:T(8,128)(2,1)}, bf16[128,1152]{1,0:T(8,128)(2,1)S(1)}, u32[]{:S(2)}, u32[]{:S(2)}) collective-permute-start(bf16[128,1152]{1,0:T(8,128)(2,1)} %get-tuple-element.192), channel_id=1, source_target_pairs={{0,16},{4,20},{8,24},{12,28},{16,32},{20,36},{24,40},{28,44},{32,4... | collective-permute-start | bytes 884744 | tf_op jit(solution)/shard_map/while/body/eval_jaxpr/ppermute | solution.py:9
  308.1 10.6 collective-permute-start.1
  308.1 15.0 %collective-permute-start = (bf16[128,1152]{1,0:T(8,128)(2,1)}, bf16[128,1152]{1,0:T(8,128)(2,1)S(1)}, u32[]{:S(2)}, u32[]{:S(2)}) collective-permute-start(bf16[128,1152]{1,0:T(8,128)(2,1)} %get-tuple-element.192), channel_id=1, source_target_pairs={{0,16},{4,20},{8,24},{12,28},{16,32},{20,36},{24,40},{28,44},{32,4... | collective-permute-start | bytes 884744 | tf_op jit(solution)/shard_map/while/body/eval_jaxpr/ppermute | solution.py:9
  329.6 10.7 collective-permute-start.1
  329.6 15.0 %collective-permute-start = (bf16[128,1152]{1,0:T(8,128)(2,1)}, bf16[128,1152]{1,0:T(8,128)(2,1)S(1)}, u32[]{:S(2)}, u32[]{:S(2)}) collective-permute-start(bf16[128,1152]{1,0:T(8,128)(2,1)} %get-tuple-element.192), channel_id=1, source_target_pairs={{0,16},{4,20},{8,24},{12,28},{16,32},{20,36},{24,40},{28,44},{32,4... | collective-permute-start | bytes 884744 | tf_op jit(solution)/shard_map/while/body/eval_jaxpr/ppermute | solution.py:9
  351.0 10.6 collective-permute-start.1
  353.1 12.9 %collective-permute-start = (bf16[128,1152]{1,0:T(8,128)(2,1)}, bf16[128,1152]{1,0:T(8,128)(2,1)S(1)}, u32[]{:S(2)}, u32[]{:S(2)}) collective-permute-start(bf16[128,1152]{1,0:T(8,128)(2,1)} %get-tuple-element.192), channel_id=1, source_target_pairs={{0,16},{4,20},{8,24},{12,28},{16,32},{20,36},{24,40},{28,44},{32,4... | collective-permute-start | bytes 884744 | tf_op jit(solution)/shard_map/while/body/eval_jaxpr/ppermute | solution.py:9
  372.4 10.7 collective-permute-start.1
  376.9 10.6 collective-permute-start
  393.9 9.7 copy-start.14
  393.9 3.4 copy-start.3
  393.9 3.4 copy-start.10
  403.6 4.4 copy-start.1
  403.6 5.5 copy-start.7
  417.3 0.7 copy-start.13
Sparse Core Ops, SparseCore 0:
  14.9 45.6 all-reduce.5
  417.5 736.9 all-reduce.7
where the time goes:
time: 1180 us; the launch traced here: 1170 us
  waiting for transfers between devices  870 us (74%)
  matrix products  145 us (12%)
  starting transfers between devices  66.5 us (6%)
  local copies, waits for them, and re-layouts  46.6 us (4%)
  other arithmetic  16.6 us (1%)
  between operations  16.1 us (1%)
    unnamed x3, waiting for transfers between devices  735 us
    ppermute x30, waiting for transfers between devices, shifted(): lax.ppermute(shard, axis, [(i, (i + by) % length) for i in range(length)])  100 us
    dot_general x19, matrix products, inner_rows(): lax.dot_general(left, right, (((0,), (0,)), ((), ())), preferred_element_...  70.7 us
    ppermute x30, starting transfers between devices, shifted(): lax.ppermute(shard, axis, [(i, (i + by) % length) for i in range(length)])  66.5 us
    dot_general x16, matrix products, signed_terms(): lax.dot_general(left, right, (((1,), (1,)), ((), ())), preferred_element_...  40 us
    while x30, local copies, waits for them, and re-layouts  36.1 us
    psum x1, waiting for transfers between devices, on_device(): feat = inputs + lax.psum(partial_out, 'mp')  34.6 us
    dot_general x15, matrix products, visit(): jnp.dot(slope_a, txt_away, preferred_element_type=jnp.float32)  28.3 us
  transfers between devices with their start and end apart: 32, of which 19 were waited for; matrix products, arithmetic and copies ran while one was open for 6% of the time, Pallas kernels for 0%

commit v1 on v0

v1 whole, which is shorter than its diff:
```python
import functools
import math

import jax
import jax.numpy as jnp
from jax import lax
from jax.experimental import pallas as pl
from jax.experimental.pallas import tpu as pltpu
from jax.sharding import PartitionSpec as P

NX, NY, NZ = 4, 4, 8
ROWS = 128
QUARTER = 32
D = 1152
HIDDEN = 1076
COLS = 288
OUT = 18
CHUNK = 24
COPIES = 160
F32, BF16 = jnp.float32, jnp.bfloat16
GELU = math.sqrt(2.0 / math.pi)


def dot(left, right):
    return jnp.dot(left, right, preferred_element_type=F32)


def dot_last(left, right):
    return lax.dot_general(left, right, (((1,), (1,)), ((), ())), preferred_element_type=F32)


def layer_norm(values, gain):
    center = values - jnp.mean(values, -1, keepdims=True)
    spread = jnp.mean(center * center, -1, keepdims=True)
    return (center * lax.rsqrt(spread + 1e-06) * gain).astype(BF16)


def unit_scale(values):
    return lax.rsqrt(jnp.sum(values * values, -1, keepdims=True) + 1e-06)


def unit_grad(values, scale, grad):
    inner = jnp.sum(values * grad, -1, keepdims=True)
    return scale * (grad - values * (scale * scale * inner))


def gelu_tanh(pre):
    return jnp.tanh(GELU * (pre + 0.044715 * pre * pre * pre))


def gelu(pre, bend):
    return (0.5 * pre * (1.0 + bend)).astype(BF16)


def gelu_slope(pre, bend):
    return 0.5 * (1.0 + bend) + 0.5 * pre * (1.0 - bend * bend) * (
        GELU * (1.0 + 3.0 * 0.044715 * pre * pre)
    )


def pair_terms(logit, sign, scale):
    arg = -sign * logit
    small = jnp.exp(-jnp.abs(arg))
    loss = jnp.maximum(arg, 0.0) + jnp.log1p(small)
    share = jnp.where(arg >= 0.0, 1.0, small) / (1.0 + small)
    return loss, -sign * share * scale


class Links:
    def __init__(self, send, recv):
        self.send, self.recv, self.started = send, recv, []

    def push(self, src, dst, device):
        at = len(self.started)
        copy = pltpu.make_async_remote_copy(
            src_ref=src,
            dst_ref=dst,
            send_sem=self.send.at[at],
            recv_sem=self.recv.at[at],
            device_id=device,
            device_id_type=pl.DeviceIdType.MESH,
        )
        copy.start()
        self.started.append(copy)
        return copy

    def drain(self):
        for copy in self.started:
            copy.wait_send()


def kernel(
    images,
    captions,
    image_gain,
    fc_in,
    fc_out,
    text_gain,
    text_head,
    ids,
    logit_scale,
    logit_bias,
    loss_out,
    in_out,
    out_out,
    head_out,
    w_in,
    w_out,
    w_head,
    own_images,
    own_captions,
    all_images,
    all_captions,
    all_dfeat,
    all_dhead,
    partial,
    d_img,
    d_txt,
    from_sibling,
    to_across,
    from_across,
    head_parts,
    head_full,
    txt_home,
    img_home,
    txt_units,
    img_units,
    sign_a,
    sign_b,
    matches,
    losses,
    pick_rows,
    pick_cols,
    act_all,
    slope_all,
    normed_t,
    text_t,
    grad_in,
    grad_out,
    grad_head,
    land_in,
    land_out,
    land_head,
    send_sems,
    recv_sems,
    load_sems,
):
    dp, mp = lax.axis_index("dp"), lax.axis_index("mp")
    z, xh, y = dp // 8, (dp // 4) % 2, dp % 4
    xl, c = mp // 2, mp % 2
    x = 2 * xh + xl
    x_lo, x_far, x_pn = 2 * xh + (1 - xl), 2 * (1 - xh) + xl, 3 - x

    def place(z_, xh_, y_, xl_, c_):
        return {"dp": z_ * 8 + xh_ * 4 + y_, "mp": xl_ * 2 + c_}

    sibling = place(z, xh, y, xl, 1 - c)
    across = place(z, xh, y, 1 - xl, c)
    diagonal = place(z, xh, y, 1 - xl, 1 - c)
    partner = place(z, 1 - xh, y, 1 - xl, c)
    y_up, y_down = place(z, xh, (y + 1) % 4, xl, c), place(z, xh, (y + 3) % 4, xl, c)
    z_up, z_down = place((z + 1) % 8, xh, y, xl, c), place((z + 7) % 8, xh, y, xl, c)

    own_slot = (x * 2 + c) * 4 + y
    loads = [
        pltpu.make_async_copy(images, own_images, load_sems.at[0]),
        pltpu.make_async_copy(captions, own_captions, load_sems.at[1]),
        pltpu.make_async_copy(images.at[mp], all_images.at[own_slot], load_sems.at[2]),
        pltpu.make_async_copy(captions.at[mp], all_captions.at[own_slot], load_sems.at[3]),
        pltpu.make_async_copy(text_head, w_head, load_sems.at[4]),
        pltpu.make_async_copy(fc_in, w_in, load_sems.at[5]),
        pltpu.make_async_copy(fc_out, w_out, load_sems.at[6]),
    ]
    for load in loads:
        load.start()

    barrier = pltpu.get_barrier_semaphore()
    peers = (sibling, across, diagonal, partner, y_up, y_down, z_up, z_down)
    for peer in peers:
        pl.semaphore_signal(barrier, inc=1, device_id=peer, device_id_type=pl.DeviceIdType.MESH)

    pos = xh * 4 + y
    row = lax.broadcasted_iota(jnp.int32, (NZ * CHUNK, D), 0)
    col = lax.broadcasted_iota(jnp.int32, (NZ * CHUNK, D), 1)
    chunk, inside = row // CHUNK, row % CHUNK
    picked = (col == chunk * (8 * OUT) + pos * OUT + inside) & (inside < OUT)
    pick_rows[...] = jnp.where(picked, 1.0, 0.0).astype(BF16)
    row = lax.broadcasted_iota(jnp.int32, (D, COLS), 0)
    col = lax.broadcasted_iota(jnp.int32, (D, COLS), 1)
    pick_cols[...] = jnp.where(row == mp * COLS + col, 1.0, 0.0).astype(BF16)

    caption = lax.broadcasted_iota(jnp.int32, (ROWS, ROWS), 0)
    match = jnp.where(caption == ids[...], 1.0, -1.0).astype(F32)
    sign_a[...] = jnp.full(sign_a.shape, -1.0, F32)
    sign_b[...] = jnp.full(sign_b.shape, -1.0, F32)
    head_full[...] = jnp.zeros(head_full.shape, F32)
    matches[...] = match.reshape(matches.shape)
    sign_a[z * 2] = matches[mp]
    matches[...] = match.T.reshape(matches.shape)
    sign_b[z * 2] = matches[mp]

    scale, bias = logit_scale[0], logit_bias[0]
    links = Links(send_sems, recv_sems)
    push = links.push
    pl.semaphore_wait(barrier, len(peers))

    class PlaneGather:
        def __init__(self, buf):
            self.buf = buf

        def column(self, x_, part=None):
            first = (x_ * 2 + c) * 4
            if part is None:
                return self.buf.at[pl.ds(first, 4)]
            return self.buf.at[pl.ds(first + 2 * part, 2)]

        def y1(self):
            own = self.buf.at[own_slot]
            self.up = push(own, own, y_up)
            self.down = push(own, own, y_down)

        def y2(self):
            first = (x * 2 + c) * 4
            self.up.wait_recv()
            half = self.buf.at[first + (y + 3) % 4, pl.ds(0, 16)]
            self.up2 = push(half, half, y_up)
            self.down.wait_recv()
            half = self.buf.at[first + (y + 1) % 4, pl.ds(16, 16)]
            self.down2 = push(half, half, y_down)

        def x1(self):
            self.up2.wait_recv()
            self.down2.wait_recv()
            own = self.column(x)
            self.sib = push(own, own, sibling)
            self.lo = push(own, own, across)
            self.pn = push(own, own, partner)

        def x2(self):
            self.lo.wait_recv()
            part = self.column(x_lo, 0)
            self.pn2 = push(part, part, partner)
            whole = self.column(x_lo)
            self.sib_lo = push(whole, whole, sibling)
            self.pn.wait_recv()
            part = self.column(x_pn, 1)
            self.lo2 = push(part, part, across)
            whole = self.column(x_pn)
            self.sib_pn = push(whole, whole, sibling)

        def x3(self):
            self.lo2.wait_recv()
            self.pn2.wait_recv()
            whole = self.column(x_far)
            self.sib_far = push(whole, whole, sibling)

        def ready(self, which):
            getattr(self, ("sib", "sib_lo", "sib_pn", "sib_far")[which]).wait_recv()

    block_x = (x, x_lo, x_pn, x_far)

    class QuadSum:
        def __init__(self, buf, at):
            self.buf, self.at = buf, at

        def s1(self):
            self.first = [
                push(self.buf.at[1 - c], from_sibling.at[self.at, 0], sibling),
                push(self.buf.at[2 + 1 - c], from_sibling.at[self.at, 1], sibling),
            ]

        def s2(self):
            for copy in self.first:
                copy.wait_recv()
            to_across[self.at] = self.buf[(1 - xl) * 2 + c] + from_sibling[self.at, 1 - xl]
            self.second = push(to_across.at[self.at], from_across.at[self.at], across)

        def total(self):
            mine = self.buf[mp] + from_sibling[self.at, xl]
            self.second.wait_recv()
            return mine + from_across[self.at]

    for load in loads[:4]:
        load.wait()
    images_plane, captions_plane = PlaneGather(all_images), PlaneGather(all_captions)
    images_plane.y1()
    captions_plane.y1()

    values = own_captions[...].reshape(ROWS, D).astype(F32)
    text_normed = layer_norm(values, text_gain[...])
    loads[4].wait()
    head_parts[mp] = dot(text_normed, w_head[...]).astype(BF16)
    head_copies = [
        push(head_parts.at[mp], head_parts.at[mp], peer) for peer in (sibling, across, diagonal)
    ]

    values = own_images[...].reshape(ROWS, D).astype(F32)
    normed = layer_norm(values, image_gain[...])
    loads[5].wait()
    pre = dot(normed, w_in[...])
    act = gelu(pre, gelu_tanh(pre))
    loads[6].wait()
    partial[...] = dot(act, w_out[...]).reshape(partial.shape)
    feat_sum = QuadSum(partial, 0)
    feat_sum.s1()
    images_plane.y2()
    captions_plane.y2()
    feat_sum.s2()

    for copy in head_copies:
        copy.wait_recv()
    for part in range(4):
        row = lax.broadcasted_iota(jnp.int32, (COLS, D), 0)
        col = lax.broadcasted_iota(jnp.int32, (COLS, D), 1)
        spread = jnp.where(col == part * COLS + row, 1.0, 0.0).astype(BF16)
        head_full[...] += dot(head_parts[part], spread).reshape(head_full.shape)
    head = head_full[...].reshape(ROWS, D)
    txt_home[...] = (head * unit_scale(head)).astype(BF16).reshape(txt_home.shape)
    txt_units[z, 0] = txt_home[mp]

    class TextRing:
        def unit(self, z_, half=None):
            slot = txt_units.at[z_ % 8, 0]
            return slot if half is None else slot.at[pl.ds(16 * half, 16)]

        def share(self, z_):
            self.shared.append(push(txt_units.at[z_ % 8, 0], txt_units.at[z_ % 8, 1], partner))

        def start(self):
            self.shared = []
            self.up = push(self.unit(z), self.unit(z), z_up)
            self.down = push(self.unit(z), self.unit(z), z_down)
            self.share(z)

        def step(self, at):
            half = at == 3
            self.up.wait_recv()
            unit = self.unit(z + 8 - at, 0 if half else None)
            self.up = push(unit, unit, z_up)
            self.share(z + 8 - at)
            self.down.wait_recv()
            unit = self.unit(z + at, 1 if half else None)
            self.down = push(unit, unit, z_down)
            self.share(z + at)

        def finish(self):
            self.up.wait_recv()
            self.down.wait_recv()
            self.share(z + 4)
            for copy in self.shared:
                copy.wait_recv()

    text_ring = TextRing()
    text_ring.start()

    feat = own_images[mp].astype(F32) + feat_sum.total()
    feat_scale = unit_scale(feat)
    img_home[mp] = (feat * feat_scale).astype(BF16)
    img_units[z, 0] = img_home[mp]
    img_partner = push(img_units.at[z, 0], img_units.at[z, 1], partner)
    img_copies = [push(img_home.at[mp], img_home.at[mp], peer) for peer in (sibling, across, diagonal)]

    class ImageRing:
        def unit(self, z_, half=None):
            return img_units.at[z_ % 8] if half is None else img_units.at[z_ % 8, half]

        def start(self):
            img_partner.wait_recv()
            self.up = push(self.unit(z), self.unit(z), z_up)
            self.down = push(self.unit(z), self.unit(z), z_down)

        def step(self, at):
            half = at == 3
            self.up.wait_recv()
            unit = self.unit(z + 8 - at, 0 if half else None)
            self.up = push(unit, unit, z_up)
            self.down.wait_recv()
            unit = self.unit(z + at, 1 if half else None)
            self.down = push(unit, unit, z_down)

        def finish(self):
            self.up.wait_recv()
            self.down.wait_recv()

    image_ring = ImageRing()
    images_plane.x1()
    image_ring.start()
    text_ring.step(1)
    captions_plane.x1()
    text_ring.step(2)
    image_ring.step(1)
    text_ring.step(3)
    images_plane.x2()
    image_ring.step(2)
    for copy in img_copies:
        copy.wait_recv()
    text_ring.finish()

    img_rows = img_home[...].reshape(ROWS, D)
    units = txt_units[...].reshape(16 * QUARTER, D)
    logit = scale * dot_last(units, img_rows) + bias
    loss, slope = pair_terms(logit, sign_a[...].reshape(16 * QUARTER, ROWS), scale)
    losses[mp] = jnp.broadcast_to(jnp.sum(loss, 0, keepdims=True), losses.shape[1:])
    loss_copies = [push(losses.at[mp], losses.at[mp], peer) for peer in (sibling, across, diagonal)]
    d_img[...] = dot(slope.T.astype(BF16), units).reshape(d_img.shape)
    img_sum = QuadSum(d_img, 1)
    img_sum.s1()
    image_ring.step(3)
    captions_plane.x2()
    images_plane.x3()
    img_sum.s2()
    captions_plane.x3()
    grad = unit_grad(feat, feat_scale, img_sum.total())
    all_dfeat[own_slot] = grad.astype(BF16)
    dfeat_plane = PlaneGather(all_dfeat)
    dfeat_plane.y1()

    image_ring.finish()
    txt_rows = txt_home[...].reshape(ROWS, D)
    units = img_units[...].reshape(16 * QUARTER, D)
    logit = scale * dot_last(units, txt_rows) + bias
    _, slope = pair_terms(logit, sign_b[...].reshape(16 * QUARTER, ROWS), scale)
    d_txt[...] = dot(slope.T.astype(BF16), units).reshape(d_txt.shape)
    txt_sum = QuadSum(d_txt, 2)
    txt_sum.s1()
    dfeat_plane.y2()
    txt_sum.s2()
    dfeat_plane.x1()
    head = head_full[mp]
    grad = unit_grad(head, unit_scale(head), txt_sum.total())
    all_dhead[own_slot] = grad.astype(BF16)
    dhead_plane = PlaneGather(all_dhead)
    dhead_plane.y1()

    def forward_block(at, carry):
        values = all_images[pl.ds(at * 8, 8)].reshape(256, D).astype(F32)
        normed = layer_norm(values, image_gain[...])
        normed_t[at] = dot_last(pick_rows[...], normed).astype(BF16)
        pre = dot(normed, w_in[...])
        bend = gelu_tanh(pre)
        act_all[at] = gelu(pre, bend)
        slope_all[at] = gelu_slope(pre, bend)
        values = all_captions[pl.ds(at * 8, 8)].reshape(256, D).astype(F32)
        text_t[at] = dot_last(pick_rows[...], layer_norm(values, text_gain[...])).astype(BF16)
        return carry

    for which in range(4):
        images_plane.ready(which)
        captions_plane.ready(which)
    lax.fori_loop(0, 4, forward_block, 0)
    dfeat_plane.x2()
    dhead_plane.y2()

    grad_in[...] = jnp.zeros(grad_in.shape, F32)
    grad_out[...] = jnp.zeros(grad_out.shape, F32)
    grad_head[...] = jnp.zeros(grad_head.shape, F32)

    def backward_block(at):
        d_feat = all_dfeat[pl.ds(at * 8, 8)].reshape(256, D)
        d_pre = (dot_last(d_feat, w_out[...]) * slope_all[at]).astype(BF16)
        d_feat_t = dot_last(pick_rows[...], d_feat).astype(BF16)
        grad_in[...] += dot(normed_t[at], d_pre).reshape(grad_in.shape)
        grad_out[...] += dot(d_feat_t, act_all[at]).reshape(grad_out.shape)

    def head_block(at, carry):
        d_head = all_dhead[pl.ds(at * 8, 8)].reshape(256, D)
        d_cols = dot(d_head, pick_cols[...]).astype(BF16)
        grad_head[...] += dot(text_t[at], d_cols).reshape(grad_head.shape)
        return carry

    dfeat_plane.ready(0)
    backward_block(block_x[0])
    dfeat_plane.x3()
    dhead_plane.x1()
    for which in range(1, 4):
        dfeat_plane.ready(which)
        backward_block(block_x[which])

    class RingSum:
        def __init__(self, buf, land, far_up):
            self.buf, self.land = buf, land
            self.first = (1, 2) if far_up else (2, 1)
            self.copy = [None, None]

        def step(self, at):
            for way in range(2):
                if at < self.first[way]:
                    continue
                dest = (z + 5 - at) % 8 if way == 0 else (z + 3 + at) % 8
                if at > self.first[way]:
                    self.copy[way].wait_recv()
                    self.buf[dest] += self.land[way, at - 2]
                self.copy[way] = push(
                    self.buf.at[dest], self.land.at[way, at - 1], (z_up, z_down)[way]
                )

        def total(self):
            for way in range(2):
                self.copy[way].wait_recv()
            return self.buf[z] + self.land[0, 3] + self.land[1, 3]

    ring_in, ring_out = RingSum(grad_in, land_in, True), RingSum(grad_out, land_out, False)
    ring_head = RingSum(grad_head, land_head, True)
    ring_in.step(1)
    ring_out.step(1)
    dhead_plane.x2()
    ring_in.step(2)
    ring_out.step(2)
    dhead_plane.x3()
    for which in range(4):
        dhead_plane.ready(which)
    lax.fori_loop(0, 4, head_block, 0)
    ring_head.step(1)
    ring_in.step(3)
    ring_out.step(3)
    ring_head.step(2)
    ring_in.step(4)
    ring_out.step(4)
    ring_head.step(3)
    ring_head.step(4)
    for copy in loss_copies:
        copy.wait_recv()
    loss_out[...] = ((losses[0] + losses[1]) + (losses[2] + losses[3]))[:1]
    in_out[...] = ring_in.total()[:OUT]
    out_out[...] = ring_out.total()[:OUT]
    head_out[...] = ring_head.total()[:OUT]
    links.drain()


def on_device(
    images,
    captions,
    image_gain,
    fc_in,
    fc_out,
    text_gain,
    text_head,
    caption_ids,
    logit_scale,
    logit_bias,
):
    whole = pl.BlockSpec(memory_space=pltpu.VMEM)
    far = pl.BlockSpec(memory_space=pl.ANY)
    scalar = pl.BlockSpec(memory_space=pltpu.SMEM)
    vmem = pltpu.VMEM
    loss, grad_in, grad_out, grad_head = pl.pallas_call(
        kernel,
        out_shape=(
            jax.ShapeDtypeStruct((1, ROWS), F32),
            jax.ShapeDtypeStruct((OUT, HIDDEN), F32),
            jax.ShapeDtypeStruct((OUT, HIDDEN), F32),
            jax.ShapeDtypeStruct((OUT, COLS), F32),
        ),
        in_specs=[far, far, whole, far, far, whole, far, whole, scalar, scalar],
        out_specs=(whole, whole, whole, whole),
        scratch_shapes=[
            vmem((D, HIDDEN), BF16),
            vmem((HIDDEN, D), BF16),
            vmem((D, COLS), BF16),
            vmem((4, QUARTER, D), BF16),
            vmem((4, QUARTER, D), BF16),
            vmem((32, QUARTER, D), BF16),
            vmem((32, QUARTER, D), BF16),
            vmem((32, QUARTER, D), BF16),
            vmem((32, QUARTER, D), BF16),
            vmem((4, QUARTER, D), F32),
            vmem((4, QUARTER, D), F32),
            vmem((4, QUARTER, D), F32),
            vmem((3, 2, QUARTER, D), F32),
            vmem((3, QUARTER, D), F32),
            vmem((3, QUARTER, D), F32),
            vmem((4, ROWS, COLS), BF16),
            vmem((4, QUARTER, D), F32),
            vmem((4, QUARTER, D), BF16),
            vmem((4, QUARTER, D), BF16),
            vmem((NZ, 2, QUARTER, D), BF16),
            vmem((NZ, 2, QUARTER, D), BF16),
            vmem((16, QUARTER, ROWS), F32),
            vmem((16, QUARTER, ROWS), F32),
            vmem((4, QUARTER, ROWS), F32),
            vmem((4, 8, ROWS), F32),
            vmem((NZ * CHUNK, D), BF16),
            vmem((D, COLS), BF16),
            vmem((4, 256, HIDDEN), BF16),
            vmem((4, 256, HIDDEN), F32),
            vmem((4, NZ * CHUNK, 256), BF16),
            vmem((4, NZ * CHUNK, 256), BF16),
            vmem((NZ, CHUNK, HIDDEN), F32),
            vmem((NZ, CHUNK, HIDDEN), F32),
            vmem((NZ, CHUNK, COLS), F32),
            vmem((2, 4, CHUNK, HIDDEN), F32),
            vmem((2, 4, CHUNK, HIDDEN), F32),
            vmem((2, 4, CHUNK, COLS), F32),
            pltpu.SemaphoreType.DMA((COPIES,)),
            pltpu.SemaphoreType.DMA((COPIES,)),
            pltpu.SemaphoreType.DMA((7,)),
        ],
        compiler_params=pltpu.CompilerParams(
            collective_id=0, has_side_effects=True, vmem_limit_bytes=56 * 1024 * 1024
        ),
        name="window",
    )(
        images.reshape(4, QUARTER, D),
        captions.reshape(4, QUARTER, D),
        image_gain.reshape(1, D),
        fc_in,
        fc_out,
        text_gain.reshape(1, D),
        text_head,
        caption_ids,
        logit_scale,
        logit_bias,
    )
    return loss.reshape(ROWS), grad_in, grad_out.T, grad_head


def solution(mesh):
    placed = (
        P("dp", None),
        P("dp", None),
        P(),
        P(None, "mp"),
        P("mp", None),
        P(),
        P(None, "mp"),
        P("dp", None),
        P(),
        P(),
    )
    return jax.shard_map(
        on_device,
        mesh=mesh,
        in_specs=placed,
        out_specs=(P("dp"), P("dp", "mp"), P("mp", "dp"), P("dp", "mp")),
        check_vma=False,
    )
```

time: 1180 us -> 135 us (0.11)
  waiting for transfers between devices: 870 us -> 0 us
  matrix products: 145 us -> 0 us
  Pallas kernels: 0 us -> 116 us
  starting transfers between devices: 66.5 us -> 0 us
  local copies, waits for them, and re-layouts: 46.6 us -> 15.8 us
  other arithmetic: 16.6 us -> 0 us
  between operations: 16.1 us -> 1.94 us
    unnamed x3 -> x0, waiting for transfers between devices: 735 us -> none
    dot_general x54 -> x0, matrix products: 145 us -> none  [the longest x19 70.7 us: inner_rows(): lax.dot_general(left, right, (((0,), (0,)), ((), ())), preferred_element_...]
    pallas_call x0 -> x1, Pallas kernels: none -> 116 us  [on_device(): pl.pallas_call(kernel, out_shape=(jax.ShapeDtypeStruct((1, ROWS), F32), j...]
    ppermute x30 -> x0, waiting for transfers between devices: 100 us -> none  [shifted(): lax.ppermute(shard, axis, [(i, (i + by) % length) for i in range(length)])]
    ppermute x30 -> x0, starting transfers between devices: 66.5 us -> none  [shifted(): lax.ppermute(shard, axis, [(i, (i + by) % length) for i in range(length)])]
    while x32 -> x0, local copies, waits for them, and re-layouts: 37.3 us -> none
    psum x1 -> x0, waiting for transfers between devices: 34.6 us -> none  [on_device(): feat = inputs + lax.psum(partial_out, 'mp')]
  transfers between devices with their start and end apart: 32 -> 0, of which waited for: 19 -> 0; matrix products, arithmetic and copies ran while one was open for 6% -> 0% of each run, Pallas kernels for 0% -> 0%
where the time goes in v1:
time: 135 us; the launch traced here: 133 us
  Pallas kernels  116 us (86%)
  local copies, waits for them, and re-layouts  15.8 us (12%)
  between operations  1.94 us (1%)
    pallas_call x1, Pallas kernels, on_device(): pl.pallas_call(kernel, out_shape=(jax.ShapeDtypeStruct((1, ROWS), F32), j...  116 us
    unnamed x6, local copies, waits for them, and re-layouts  13.2 us

profile of v1, /device:TPU:32, one launch (start us, length us, event | category | flops | bytes accessed | tf_op | source)
XLA Modules:
  0.0 133.4 jit_solution(17680380020402057238)
XLA Ops:
  1.9 1.3 reshape.25.image_gain
  3.2 1.3 reshape.26.text_gain
  4.5 2.3 %copy.15.text_head = bf16[1152,288]{1,0:T(8,128)(2,1)} copy(bf16[1152,288]{0,1:T(8,128)(2,1)} %param.16) | data formatting | bytes 1327104 | tf_op args[6]
  6.9 5.2 %copy.14.fc_in = bf16[1152,1076]{1,0:T(8,128)(2,1)} copy(bf16[1152,1076]{0,1:T(8,128)(2,1)} %param.13) | data formatting | bytes 4958208 | tf_op args[3]
  12.0 115.7 %window.1 = (f32[1,128]{1,0:T(1,128)}, f32[18,1076]{1,0:T(8,128)}, f32[18,1076]{1,0:T(8,128)}, f32[18,288]{1,0:T(8,128)}) custom-call(bf16[4,32,1152]{2,1,0:T(8,128)(2,1)} %bitcast.4, bf16[4,32,1152]{2,1,0:T(8,128)(2,1)} %bitcast.5, f32[1,1152]{1,0:T(1,128)} %reshape.25.image_gain, bf16[1152,1076]{1,0:T(8,128)(2,1)} %copy.14.fc_in, ...), custom_call_target="tpu_custom_call" | custom-call | tf_op jit(solution)/shard_map/window/pallas_call | solution.py:546
  127.7 1.2 copy.22
  128.9 1.5 %copy.23 = f32[18,1076]{1,0:T(8,128)} copy(f32[18,1076]{1,0:T(8,128)} %get-tuple-element.17) | data formatting | bytes 154944
  130.5 1.5 %copy.24 = f32[1076,18]{0,1:T(8,128)} copy(f32[1076,18]{0,1:T(8,128)} %bitcast.6) | data formatting | bytes 154944
  132.0 1.4 %copy.25 = f32[18,288]{1,0:T(8,128)} copy(f32[18,288]{1,0:T(8,128)} %get-tuple-element.19) | data formatting | bytes 41472

commit v2 on v1

--- a/solution.py
+++ b/solution.py
@@ -16,6 +16,7 @@
 COLS = 288
 OUT = 18
 CHUNK = 24
+HEAD_CHUNK = 32
 COPIES = 160
 F32, BF16 = jnp.float32, jnp.bfloat16
 GELU = math.sqrt(2.0 / math.pi)
@@ -138,8 +139,10 @@
     grad_in,
     grad_out,
     grad_head,
-    land_in,
-    land_out,
+    packed,
+    stage_main,
+    stage_head,
+    land_main,
     land_head,
     send_sems,
     recv_sems,
@@ -149,7 +152,8 @@
     z, xh, y = dp // 8, (dp // 4) % 2, dp % 4
     xl, c = mp // 2, mp % 2
     x = 2 * xh + xl
-    x_lo, x_far, x_pn = 2 * xh + (1 - xl), 2 * (1 - xh) + xl, 3 - x
+    x_lo, x_pn = 2 * xh + (1 - xl), 3 - x
+    y_above, y_below, y_far = (y + 1) % 4, (y + 3) % 4, (y + 2) % 4
 
     def place(z_, xh_, y_, xl_, c_):
         return {"dp": z_ * 8 + xh_ * 4 + y_, "mp": xl_ * 2 + c_}
@@ -158,10 +162,10 @@
     across = place(z, xh, y, 1 - xl, c)
     diagonal = place(z, xh, y, 1 - xl, 1 - c)
     partner = place(z, 1 - xh, y, 1 - xl, c)
-    y_up, y_down = place(z, xh, (y + 1) % 4, xl, c), place(z, xh, (y + 3) % 4, xl, c)
+    y_up, y_down = place(z, xh, y_above, xl, c), place(z, xh, y_below, xl, c)
     z_up, z_down = place((z + 1) % 8, xh, y, xl, c), place((z + 7) % 8, xh, y, xl, c)
 
-    own_slot = (x * 2 + c) * 4 + y
+    own_slot = (y * 2 + c) * 4 + x
     loads = [
         pltpu.make_async_copy(images, own_images, load_sems.at[0]),
         pltpu.make_async_copy(captions, own_captions, load_sems.at[1]),
@@ -179,26 +183,6 @@
     for peer in peers:
         pl.semaphore_signal(barrier, inc=1, device_id=peer, device_id_type=pl.DeviceIdType.MESH)
 
-    pos = xh * 4 + y
-    row = lax.broadcasted_iota(jnp.int32, (NZ * CHUNK, D), 0)
-    col = lax.broadcasted_iota(jnp.int32, (NZ * CHUNK, D), 1)
-    chunk, inside = row // CHUNK, row % CHUNK
-    picked = (col == chunk * (8 * OUT) + pos * OUT + inside) & (inside < OUT)
-    pick_rows[...] = jnp.where(picked, 1.0, 0.0).astype(BF16)
-    row = lax.broadcasted_iota(jnp.int32, (D, COLS), 0)
-    col = lax.broadcasted_iota(jnp.int32, (D, COLS), 1)
-    pick_cols[...] = jnp.where(row == mp * COLS + col, 1.0, 0.0).astype(BF16)
-
-    caption = lax.broadcasted_iota(jnp.int32, (ROWS, ROWS), 0)
-    match = jnp.where(caption == ids[...], 1.0, -1.0).astype(F32)
-    sign_a[...] = jnp.full(sign_a.shape, -1.0, F32)
-    sign_b[...] = jnp.full(sign_b.shape, -1.0, F32)
-    head_full[...] = jnp.zeros(head_full.shape, F32)
-    matches[...] = match.reshape(matches.shape)
-    sign_a[z * 2] = matches[mp]
-    matches[...] = match.T.reshape(matches.shape)
-    sign_b[z * 2] = matches[mp]
-
     scale, bias = logit_scale[0], logit_bias[0]
     links = Links(send_sems, recv_sems)
     push = links.push
@@ -208,56 +192,56 @@
         def __init__(self, buf):
             self.buf = buf
 
-        def column(self, x_, part=None):
-            first = (x_ * 2 + c) * 4
+        def group(self, y_, part=None):
+            first = (y_ * 2 + c) * 4
             if part is None:
                 return self.buf.at[pl.ds(first, 4)]
             return self.buf.at[pl.ds(first + 2 * part, 2)]
 
+        def x1(self):
+            own = self.buf.at[own_slot]
+            self.lo = push(own, own, across)
+            self.pn = push(own, own, partner)
+
+        def x2(self):
+            first = (y * 2 + c) * 4
+            self.lo.wait_recv()
+            half = self.buf.at[first + x_lo, pl.ds(0, 16)]
+            self.pn2 = push(half, half, partner)
+            self.pn.wait_recv()
+            half = self.buf.at[first + x_pn, pl.ds(16, 16)]
+            self.lo2 = push(half, half, across)
+
         def y1(self):
-            own = self.buf.at[own_slot]
+            self.pn2.wait_recv()
+            self.lo2.wait_recv()
+            own = self.group(y)
+            self.sib = push(own, own, sibling)
             self.up = push(own, own, y_up)
             self.down = push(own, own, y_down)
 
         def y2(self):
-            first = (x * 2 + c) * 4
             self.up.wait_recv()
-            half = self.buf.at[first + (y + 3) % 4, pl.ds(0, 16)]
-            self.up2 = push(half, half, y_up)
+            part = self.group(y_below, 0)
+            self.up2 = push(part, part, y_up)
+            whole = self.group(y_below)
+            self.sib_up = push(whole, whole, sibling)
             self.down.wait_recv()
-            half = self.buf.at[first + (y + 1) % 4, pl.ds(16, 16)]
-            self.down2 = push(half, half, y_down)
-
-        def x1(self):
+            part = self.group(y_above, 1)
+            self.down2 = push(part, part, y_down)
+            whole = self.group(y_above)
+            self.sib_down = push(whole, whole, sibling)
+
+        def y3(self):
             self.up2.wait_recv()
             self.down2.wait_recv()
-            own = self.column(x)
-            self.sib = push(own, own, sibling)
-            self.lo = push(own, own, across)
-            self.pn = push(own, own, partner)
-
-        def x2(self):
-            self.lo.wait_recv()
-            part = self.column(x_lo, 0)
-            self.pn2 = push(part, part, partner)
-            whole = self.column(x_lo)
-            self.sib_lo = push(whole, whole, sibling)
-            self.pn.wait_recv()
-            part = self.column(x_pn, 1)
-            self.lo2 = push(part, part, across)
-            whole = self.column(x_pn)
-            self.sib_pn = push(whole, whole, sibling)
-
-        def x3(self):
-            self.lo2.wait_recv()
-            self.pn2.wait_recv()
-            whole = self.column(x_far)
+            whole = self.group(y_far)
             self.sib_far = push(whole, whole, sibling)
 
         def ready(self, which):
-            getattr(self, ("sib", "sib_lo", "sib_pn", "sib_far")[which]).wait_recv()
-
-    block_x = (x, x_lo, x_pn, x_far)
+            getattr(self, ("sib", "sib_up", "sib_down", "sib_far")[which]).wait_recv()
+
+    blocks = (y, y_below, y_above, y_far)
 
     class QuadSum:
         def __init__(self, buf, at):
@@ -283,38 +267,61 @@
     for load in loads[:4]:
         load.wait()
     images_plane, captions_plane = PlaneGather(all_images), PlaneGather(all_captions)
-    images_plane.y1()
-    captions_plane.y1()
+    images_plane.x1()
+    captions_plane.x1()
 
     values = own_captions[...].reshape(ROWS, D).astype(F32)
-    text_normed = layer_norm(values, text_gain[...])
+    text_normed = layer_norm(values, text_gain[...].reshape(1, D))
     loads[4].wait()
-    head_parts[mp] = dot(text_normed, w_head[...]).astype(BF16)
+    head_parts[mp] = dot_last(text_normed, w_head[...]).astype(BF16)
     head_copies = [
         push(head_parts.at[mp], head_parts.at[mp], peer) for peer in (sibling, across, diagonal)
     ]
 
+    images_plane.x2()
+    captions_plane.x2()
+
     values = own_images[...].reshape(ROWS, D).astype(F32)
-    normed = layer_norm(values, image_gain[...])
+    normed = layer_norm(values, image_gain[...].reshape(1, D))
     loads[5].wait()
-    pre = dot(normed, w_in[...])
+    pre = dot_last(normed, w_in[...])
     act = gelu(pre, gelu_tanh(pre))
     loads[6].wait()
     partial[...] = dot(act, w_out[...]).reshape(partial.shape)
     feat_sum = QuadSum(partial, 0)
     feat_sum.s1()
-    images_plane.y2()
-    captions_plane.y2()
+    images_plane.y1()
+    captions_plane.y1()
+
+    chunk = lax.broadcasted_iota(jnp.int32, (NZ, CHUNK, D), 0)
+    inside = lax.broadcasted_iota(jnp.int32, (NZ, CHUNK, D), 1)
+    col = lax.broadcasted_iota(jnp.int32, (NZ, CHUNK, D), 2)
+    pos = xh * 4 + y
+    picked = (col == chunk * (8 * OUT) + pos * OUT + inside) & (inside < OUT)
+    pick_rows[...] = jnp.where(picked, 1.0, 0.0).reshape(NZ * CHUNK, D).astype(BF16)
+    row = lax.broadcasted_iota(jnp.int32, (D, COLS), 0)
+    col = lax.broadcasted_iota(jnp.int32, (D, COLS), 1)
+    pick_cols[...] = jnp.where(row == mp * COLS + col, 1.0, 0.0).astype(BF16)
+
+    caption = lax.broadcasted_iota(jnp.int32, (ROWS, ROWS), 0)
+    match = jnp.where(caption == ids[...], 1.0, -1.0).astype(F32)
+    sign_a[...] = jnp.full(sign_a.shape, -1.0, F32)
+    sign_b[...] = jnp.full(sign_b.shape, -1.0, F32)
+    matches[...] = match.reshape(matches.shape)
+    sign_a[z * 2] = matches[mp]
+    matches[...] = match.T.reshape(matches.shape)
+    sign_b[z * 2] = matches[mp]
+    grad_in[...] = jnp.zeros(grad_in.shape, F32)
+    grad_out[...] = jnp.zeros(grad_out.shape, F32)
+    grad_head[...] = jnp.zeros(grad_head.shape, F32)
+    packed[...] = jnp.zeros(packed.shape, F32)
+
     feat_sum.s2()
 
     for copy in head_copies:
         copy.wait_recv()
-    for part in range(4):
-        row = lax.broadcasted_iota(jnp.int32, (COLS, D), 0)
-        col = lax.broadcasted_iota(jnp.int32, (COLS, D), 1)
-        spread = jnp.where(col == part * COLS + row, 1.0, 0.0).astype(BF16)
-        head_full[...] += dot(head_parts[part], spread).reshape(head_full.shape)
-    head = head_full[...].reshape(ROWS, D)
+    head = jnp.concatenate([head_parts[part].astype(F32) for part in range(4)], 1)
+    head_full[...] = head.reshape(head_full.shape)
     txt_home[...] = (head * unit_scale(head)).astype(BF16).reshape(txt_home.shape)
     txt_units[z, 0] = txt_home[mp]
 
@@ -382,16 +389,35 @@
             self.up.wait_recv()
             self.down.wait_recv()
 
+    def forward_block(which):
+        at = blocks[which]
+        images_plane.ready(which)
+        values = all_images[pl.ds(at * 8, 8)].reshape(256, D).astype(F32)
+        normed = layer_norm(values, image_gain[...].reshape(1, D))
+        normed_t[at] = dot_last(pick_rows[...], normed).astype(BF16)
+        pre = dot_last(normed, w_in[...])
+        bend = gelu_tanh(pre)
+        act_all[at] = gelu(pre, bend)
+        slope_all[at] = gelu_slope(pre, bend)
+        captions_plane.ready(which)
+        values = all_captions[pl.ds(at * 8, 8)].reshape(256, D).astype(F32)
+        text_normed = layer_norm(values, text_gain[...].reshape(1, D))
+        text_t[at] = dot_last(pick_rows[...], text_normed).astype(BF16)
+
     image_ring = ImageRing()
-    images_plane.x1()
     image_ring.start()
     text_ring.step(1)
-    captions_plane.x1()
+    images_plane.y2()
+    captions_plane.y2()
+    forward_block(0)
     text_ring.step(2)
     image_ring.step(1)
+    forward_block(1)
     text_ring.step(3)
-    images_plane.x2()
     image_ring.step(2)
+    images_plane.y3()
+    captions_plane.y3()
+    forward_block(2)
     for copy in img_copies:
         copy.wait_recv()
     text_ring.finish()
@@ -406,14 +432,12 @@
     img_sum = QuadSum(d_img, 1)
     img_sum.s1()
     image_ring.step(3)
-    captions_plane.x2()
-    images_plane.x3()
     img_sum.s2()
-    captions_plane.x3()
+    forward_block(3)
     grad = unit_grad(feat, feat_scale, img_sum.total())
     all_dfeat[own_slot] = grad.astype(BF16)
     dfeat_plane = PlaneGather(all_dfeat)
-    dfeat_plane.y1()
+    dfeat_plane.x1()
 
     image_ring.finish()
     txt_rows = txt_home[...].reshape(ROWS, D)
@@ -423,37 +447,14 @@
     d_txt[...] = dot(slope.T.astype(BF16), units).reshape(d_txt.shape)
     txt_sum = QuadSum(d_txt, 2)
     txt_sum.s1()
-    dfeat_plane.y2()
+    dfeat_plane.x2()
     txt_sum.s2()
-    dfeat_plane.x1()
+    dfeat_plane.y1()
     head = head_full[mp]
     grad = unit_grad(head, unit_scale(head), txt_sum.total())
     all_dhead[own_slot] = grad.astype(BF16)
     dhead_plane = PlaneGather(all_dhead)
-    dhead_plane.y1()
-
-    def forward_block(at, carry):
-        values = all_images[pl.ds(at * 8, 8)].reshape(256, D).astype(F32)
-        normed = layer_norm(values, image_gain[...])
-        normed_t[at] = dot_last(pick_rows[...], normed).astype(BF16)
-        pre = dot(normed, w_in[...])
-        bend = gelu_tanh(pre)
-        act_all[at] = gelu(pre, bend)
-        slope_all[at] = gelu_slope(pre, bend)
-        values = all_captions[pl.ds(at * 8, 8)].reshape(256, D).astype(F32)
-        text_t[at] = dot_last(pick_rows[...], layer_norm(values, text_gain[...])).astype(BF16)
-        return carry
-
-    for which in range(4):
-        images_plane.ready(which)
-        captions_plane.ready(which)
-    lax.fori_loop(0, 4, forward_block, 0)
-    dfeat_plane.x2()
-    dhead_plane.y2()
-
-    grad_in[...] = jnp.zeros(grad_in.shape, F32)
-    grad_out[...] = jnp.zeros(grad_out.shape, F32)
-    grad_head[...] = jnp.zeros(grad_head.shape, F32)
+    dhead_plane.x1()
 
     def backward_block(at):
         d_feat = all_dfeat[pl.ds(at * 8, 8)].reshape(256, D)
@@ -462,23 +463,38 @@
         grad_in[...] += dot(normed_t[at], d_pre).reshape(grad_in.shape)
         grad_out[...] += dot(d_feat_t, act_all[at]).reshape(grad_out.shape)
 
-    def head_block(at, carry):
+    def head_block(at):
         d_head = all_dhead[pl.ds(at * 8, 8)].reshape(256, D)
         d_cols = dot(d_head, pick_cols[...]).astype(BF16)
-        grad_head[...] += dot(text_t[at], d_cols).reshape(grad_head.shape)
-        return carry
+        grad = dot(text_t[at], d_cols).reshape(NZ, CHUNK, COLS)
+        grad_head[:, pl.ds(0, CHUNK)] += grad
 
     dfeat_plane.ready(0)
-    backward_block(block_x[0])
-    dfeat_plane.x3()
-    dhead_plane.x1()
-    for which in range(1, 4):
-        dfeat_plane.ready(which)
-        backward_block(block_x[which])
+    backward_block(blocks[0])
+    dhead_plane.x2()
+    dfeat_plane.y2()
+    dfeat_plane.ready(1)
+    backward_block(blocks[1])
+    dhead_plane.y1()
+    dfeat_plane.ready(2)
+    backward_block(blocks[2])
+    dfeat_plane.y3()
+    dhead_plane.y2()
+    dfeat_plane.ready(3)
+    backward_block(blocks[3])
+
+    def pack(at):
+        for part in range(3):
+            width = min(384, HIDDEN - 384 * part)
+            lanes = pl.ds(384 * part, width)
+            packed[at, pl.ds(OUT * part, OUT), pl.ds(0, width)] = grad_in[at, pl.ds(0, OUT), lanes]
+            packed[at, pl.ds(OUT * (part + 3), OUT), pl.ds(0, width)] = grad_out[
+                at, pl.ds(0, OUT), lanes
+            ]
 
     class RingSum:
-        def __init__(self, buf, land, far_up):
-            self.buf, self.land = buf, land
+        def __init__(self, buf, rows, stage, land, far_up):
+            self.buf, self.rows, self.stage, self.land = buf, rows, stage, land
             self.first = (1, 2) if far_up else (2, 1)
             self.copy = [None, None]
 
@@ -487,44 +503,68 @@
                 if at < self.first[way]:
                     continue
                 dest = (z + 5 - at) % 8 if way == 0 else (z + 3 + at) % 8
+                term = self.buf[dest, self.rows]
                 if at > self.first[way]:
                     self.copy[way].wait_recv()
-                    self.buf[dest] += self.land[way, at - 2]
+                    term += self.land[way, at - 2, self.rows].astype(F32)
+                self.stage[way, at - 1, self.rows] = term.astype(BF16)
                 self.copy[way] = push(
-                    self.buf.at[dest], self.land.at[way, at - 1], (z_up, z_down)[way]
+                    self.stage.at[way, at - 1, self.rows],
+                    self.land.at[way, at - 1, self.rows],
+                    (z_up, z_down)[way],
                 )
 
         def total(self):
             for way in range(2):
                 self.copy[way].wait_recv()
-            return self.buf[z] + self.land[0, 3] + self.land[1, 3]
-
-    ring_in, ring_out = RingSum(grad_in, land_in, True), RingSum(grad_out, land_out, False)
-    ring_head = RingSum(grad_head, land_head, True)
-    ring_in.step(1)
-    ring_out.step(1)
-    dhead_plane.x2()
-    ring_in.step(2)
-    ring_out.step(2)
-    dhead_plane.x3()
+            away = [self.land[way, 3, self.rows].astype(F32) for way in range(2)]
+            return self.buf[z, self.rows] + away[0] + away[1]
+
+    first, second = pl.ds(0, 64), pl.ds(64, 48)
+    rings = (
+        RingSum(packed, first, stage_main, land_main, True),
+        RingSum(packed, second, stage_main, land_main, False),
+    )
+    ring_head = RingSum(grad_head, pl.ds(0, HEAD_CHUNK), stage_head, land_head, True)
+    pack((z + 4) % 8)
+    for ring in rings:
+        ring.step(1)
+    pack((z + 3) % 8)
+    pack((z + 5) % 8)
+    for ring in rings:
+        ring.step(2)
+    pack((z + 2) % 8)
+    pack((z + 6) % 8)
+    dhead_plane.y3()
+    for ring in rings:
+        ring.step(3)
+    pack((z + 1) % 8)
+    pack((z + 7) % 8)
+    pack(z)
+    for ring in rings:
+        ring.step(4)
     for which in range(4):
         dhead_plane.ready(which)
-    lax.fori_loop(0, 4, head_block, 0)
-    ring_head.step(1)
-    ring_in.step(3)
-    ring_out.step(3)
-    ring_head.step(2)
-    ring_in.step(4)
-    ring_out.step(4)
-    ring_head.step(3)
-    ring_head.step(4)
+        head_block(blocks[which])
+    for at in range(1, 5):
+        ring_head.step(at)
     for copy in loss_copies:
         copy.wait_recv()
     loss_out[...] = ((losses[0] + losses[1]) + (losses[2] + losses[3]))[:1]
-    in_out[...] = ring_in.total()[:OUT]
-    out_out[...] = ring_out.total()[:OUT]
+    packed[z, first] = rings[0].total()
+    packed[z, second] = rings[1].total()
+    for part in range(3):
+        width = min(384, HIDDEN - 384 * part)
+        lanes = pl.ds(384 * part, width)
+        in_out[:, lanes] = packed[z, pl.ds(OUT * part, OUT), pl.ds(0, width)]
+        out_out[:, lanes] = packed[z, pl.ds(OUT * (part + 3), OUT), pl.ds(0, width)]
     head_out[...] = ring_head.total()[:OUT]
     links.drain()
+
+
+def copy_out(*refs):
+    for src, dst in zip(refs[:4], refs[4:]):
+        dst[...] = src[...]
 
 
 def on_device(
@@ -543,20 +583,21 @@
     far = pl.BlockSpec(memory_space=pl.ANY)
     scalar = pl.BlockSpec(memory_space=pltpu.SMEM)
     vmem = pltpu.VMEM
-    loss, grad_in, grad_out, grad_head = pl.pallas_call(
+    results = (
+        jax.ShapeDtypeStruct((1, ROWS), F32),
+        jax.ShapeDtypeStruct((OUT, HIDDEN), F32),
+        jax.ShapeDtypeStruct((OUT, HIDDEN), F32),
+        jax.ShapeDtypeStruct((OUT, COLS), F32),
+    )
+    found = pl.pallas_call(
         kernel,
-        out_shape=(
-            jax.ShapeDtypeStruct((1, ROWS), F32),
-            jax.ShapeDtypeStruct((OUT, HIDDEN), F32),
-            jax.ShapeDtypeStruct((OUT, HIDDEN), F32),
-            jax.ShapeDtypeStruct((OUT, COLS), F32),
-        ),
+        out_shape=results,
         in_specs=[far, far, whole, far, far, whole, far, whole, scalar, scalar],
         out_specs=(whole, whole, whole, whole),
         scratch_shapes=[
-            vmem((D, HIDDEN), BF16),
             vmem((HIDDEN, D), BF16),
-            vmem((D, COLS), BF16),
+            vmem((HIDDEN, D), BF16),
+            vmem((COLS, D), BF16),
             vmem((4, QUARTER, D), BF16),
             vmem((4, QUARTER, D), BF16),
             vmem((32, QUARTER, D), BF16),
@@ -587,10 +628,12 @@
             vmem((4, NZ * CHUNK, 256), BF16),
             vmem((NZ, CHUNK, HIDDEN), F32),
             vmem((NZ, CHUNK, HIDDEN), F32),
-            vmem((NZ, CHUNK, COLS), F32),
-            vmem((2, 4, CHUNK, HIDDEN), F32),
-            vmem((2, 4, CHUNK, HIDDEN), F32),
-            vmem((2, 4, CHUNK, COLS), F32),
+            vmem((NZ, HEAD_CHUNK, COLS), F32),
+            vmem((NZ, 112, 384), F32),
+            vmem((2, 4, 112, 384), BF16),
+            vmem((2, 4, HEAD_CHUNK, COLS), BF16),
+            vmem((2, 4, 112, 384), BF16),
+            vmem((2, 4, HEAD_CHUNK, COLS), BF16),
             pltpu.SemaphoreType.DMA((COPIES,)),
             pltpu.SemaphoreType.DMA((COPIES,)),
             pltpu.SemaphoreType.DMA((7,)),
@@ -602,15 +645,22 @@
     )(
         images.reshape(4, QUARTER, D),
         captions.reshape(4, QUARTER, D),
-        image_gain.reshape(1, D),
-        fc_in,
+        image_gain,
+        fc_in.T,
         fc_out,
-        text_gain.reshape(1, D),
-        text_head,
+        text_gain,
+        text_head.T,
         caption_ids,
         logit_scale,
         logit_bias,
     )
+    loss, grad_in, grad_out, grad_head = pl.pallas_call(
+        copy_out,
+        out_shape=results,
+        in_specs=[whole] * 4,
+        out_specs=(whole,) * 4,
+        name="results",
+    )(*found)
     return loss.reshape(ROWS), grad_in, grad_out.T, grad_head
 
 

time: 135 us -> 118 us (0.87)
  local copies, waits for them, and re-layouts: 15.8 us -> 0 us
    unnamed x6 -> x0, local copies, waits for them, and re-layouts: 13.2 us -> none
    reshape x2 -> x0, local copies, waits for them, and re-layouts: 2.59 us -> none  [the longest x1 1.29 us: on_device(): image_gain.reshape(1, D)]
    pallas_call x1 -> x2, Pallas kernels: 116 us -> 115 us  [the longest x1 113 us: on_device(): pl.pallas_call(kernel, out_shape=results, in_specs=[far, far, whole, far,...]
where the time goes in v2:
time: 118 us; the launch traced here: 117 us
  Pallas kernels  115 us (97%)
  between operations  1.93 us (2%)
    pallas_call x1, Pallas kernels, on_device(): pl.pallas_call(kernel, out_shape=results, in_specs=[far, far, whole, far,...  113 us

profile of v2, /device:TPU:32, one launch (start us, length us, event | category | flops | bytes accessed | tf_op | source)
XLA Modules:
  0.0 116.9 jit_solution(11297911886242774721)
XLA Ops:
  1.9 113.3 %window.1 = (f32[1,128]{1,0:T(1,128)}, f32[18,1076]{1,0:T(8,128)}, f32[18,1076]{1,0:T(8,128)}, f32[18,288]{1,0:T(8,128)}) custom-call(bf16[4,32,1152]{2,1,0:T(8,128)(2,1)} %bitcast.8, bf16[4,32,1152]{2,1,0:T(8,128)(2,1)} %bitcast.9, f32[1152]{0:T(1024)} %image_gain.1, bf16[1076,1152]{1,0:T(8,128)(2,1)} %bitcast.6, bf16[1076,1152]{1,0:T(8,128)(2,1)} %fc_out.1, ...), custom_call_target="tpu_custom_call" | custom-call | tf_op jit(solution)/shard_map/window/pallas_call | solution.py:592
  115.2 1.7 %results.1 = (f32[1,128]{1,0:T(1,128)}, f32[18,1076]{1,0:T(8,128)}, f32[18,1076]{1,0:T(8,128)}, f32[18,288]{1,0:T(8,128)}) custom-call(f32[1,128]{1,0:T(1,128)} %get-tuple-element.12.refs_0_, f32[18,1076]{1,0:T(8,128)} %get-tuple-element.13.refs_1_, f32[18,1076]{1,0:T(8,128)} %get-tuple-element.14.refs_2_, f32[18,288]{1,0:T(8,128)} %get-tuple-element.15.refs_3_), custom_call_target="tpu_custom_call" | custom-call | tf_op jit(solution)/shard_map/results/pallas_call | solution.py:657

commit v3 on v2

--- a/solution.py
+++ b/solution.py
@@ -17,7 +17,7 @@
 OUT = 18
 CHUNK = 24
 HEAD_CHUNK = 32
-COPIES = 160
+COPIES = 200
 F32, BF16 = jnp.float32, jnp.bfloat16
 GELU = math.sqrt(2.0 / math.pi)
 
@@ -165,15 +165,27 @@
     y_up, y_down = place(z, xh, y_above, xl, c), place(z, xh, y_below, xl, c)
     z_up, z_down = place((z + 1) % 8, xh, y, xl, c), place((z + 7) % 8, xh, y, xl, c)
 
-    own_slot = (y * 2 + c) * 4 + x
+    x_axis = dict(
+        at=(x, x_lo, x_pn, 3 - x_lo), to=(across, partner), on=(partner, across)
+    )
+    y_axis = dict(
+        at=(y, y_below, y_above, y_far), to=(y_up, y_down), on=(y_up, y_down)
+    )
+
+    def own_slot(half):
+        return (y * 2 + c) * 4 + x if half == 0 else (x * 2 + c) * 4 + y
+
+    pairs = [(images, own_images), (captions, own_captions)]
+    for src, dst in ((images, all_images), (captions, all_captions)):
+        for half in range(2):
+            pairs.append((src.at[mp, pl.ds(16 * half, 16)], dst.at[half, own_slot(half)]))
+    pairs.append((text_head, w_head))
+    for src, dst in ((fc_in, w_in), (fc_out, w_out)):
+        for part in range(3):
+            lanes = pl.ds(384 * part, 384)
+            pairs.append((src.at[:, lanes], dst.at[:, lanes]))
     loads = [
-        pltpu.make_async_copy(images, own_images, load_sems.at[0]),
-        pltpu.make_async_copy(captions, own_captions, load_sems.at[1]),
-        pltpu.make_async_copy(images.at[mp], all_images.at[own_slot], load_sems.at[2]),
-        pltpu.make_async_copy(captions.at[mp], all_captions.at[own_slot], load_sems.at[3]),
-        pltpu.make_async_copy(text_head, w_head, load_sems.at[4]),
-        pltpu.make_async_copy(fc_in, w_in, load_sems.at[5]),
-        pltpu.make_async_copy(fc_out, w_out, load_sems.at[6]),
+        pltpu.make_async_copy(src, dst, load_sems.at[at]) for at, (src, dst) in enumerate(pairs)
     ]
     for load in loads:
         load.start()
@@ -188,60 +200,72 @@
     push = links.push
     pl.semaphore_wait(barrier, len(peers))
 
+    class HalfGather:
+        def __init__(self, buf, half, lead, follow):
+            self.buf, self.half, self.lead, self.follow = buf, half, lead, follow
+
+        def slot(self, which, lanes):
+            at = (self.follow["at"][0] * 2 + c) * 4 + self.lead["at"][which]
+            return self.buf.at[self.half, at, :, lanes]
+
+        def group(self, which, part=None):
+            first = (self.follow["at"][which] * 2 + c) * 4
+            if part is None:
+                return self.buf.at[self.half, pl.ds(first, 4)]
+            return self.buf.at[self.half, pl.ds(first + 2 * part, 2)]
+
+        def a1(self):
+            own = self.slot(0, pl.ds(0, D))
+            self.near = [push(own, own, self.lead["to"][way]) for way in range(2)]
+
+        def a2(self):
+            self.next = []
+            for way in range(2):
+                self.near[way].wait_recv()
+                part = self.slot(1 + way, (pl.ds(0, 640), pl.ds(640, 512))[way])
+                self.next.append(push(part, part, self.lead["on"][way]))
+
+        def b1(self):
+            for copy in self.next:
+                copy.wait_recv()
+            own = self.group(0)
+            self.sib = [push(own, own, sibling)]
+            self.near = [push(own, own, self.follow["to"][way]) for way in range(2)]
+
+        def b2(self):
+            self.next = []
+            for way in range(2):
+                self.near[way].wait_recv()
+                part = self.group(1 + way, way)
+                self.next.append(push(part, part, self.follow["on"][way]))
+                whole = self.group(1 + way)
+                self.sib.append(push(whole, whole, sibling))
+
+        def b3(self):
+            for copy in self.next:
+                copy.wait_recv()
+            whole = self.group(3)
+            self.sib.append(push(whole, whole, sibling))
+
     class PlaneGather:
         def __init__(self, buf):
             self.buf = buf
-
-        def group(self, y_, part=None):
-            first = (y_ * 2 + c) * 4
-            if part is None:
-                return self.buf.at[pl.ds(first, 4)]
-            return self.buf.at[pl.ds(first + 2 * part, 2)]
-
-        def x1(self):
-            own = self.buf.at[own_slot]
-            self.lo = push(own, own, across)
-            self.pn = push(own, own, partner)
-
-        def x2(self):
-            first = (y * 2 + c) * 4
-            self.lo.wait_recv()
-            half = self.buf.at[first + x_lo, pl.ds(0, 16)]
-            self.pn2 = push(half, half, partner)
-            self.pn.wait_recv()
-            half = self.buf.at[first + x_pn, pl.ds(16, 16)]
-            self.lo2 = push(half, half, across)
-
-        def y1(self):
-            self.pn2.wait_recv()
-            self.lo2.wait_recv()
-            own = self.group(y)
-            self.sib = push(own, own, sibling)
-            self.up = push(own, own, y_up)
-            self.down = push(own, own, y_down)
-
-        def y2(self):
-            self.up.wait_recv()
-            part = self.group(y_below, 0)
-            self.up2 = push(part, part, y_up)
-            whole = self.group(y_below)
-            self.sib_up = push(whole, whole, sibling)
-            self.down.wait_recv()
-            part = self.group(y_above, 1)
-            self.down2 = push(part, part, y_down)
-            whole = self.group(y_above)
-            self.sib_down = push(whole, whole, sibling)
-
-        def y3(self):
-            self.up2.wait_recv()
-            self.down2.wait_recv()
-            whole = self.group(y_far)
-            self.sib_far = push(whole, whole, sibling)
-
-        def ready(self, which):
-            getattr(self, ("sib", "sib_up", "sib_down", "sib_far")[which]).wait_recv()
-
-    blocks = (y, y_below, y_above, y_far)
+            self.halves = (
+                HalfGather(buf, 0, x_axis, y_axis),
+                HalfGather(buf, 1, y_axis, x_axis),
+            )
+
+        def stage(self, name):
+            for half in self.halves:
+                getattr(half, name)()
+
+        def block(self, which):
+            rows = []
+            for half in self.halves:
+                half.sib[which].wait_recv()
+                first = half.follow["at"][which] * 8
+                rows.append(self.buf[half.half, pl.ds(first, 8)].reshape(128, D))
+            return jnp.concatenate(rows, 0)
 
     class QuadSum:
         def __init__(self, buf, at):
@@ -256,42 +280,45 @@
         def s2(self):
             for copy in self.first:
                 copy.wait_recv()
-            to_across[self.at] = self.buf[(1 - xl) * 2 + c] + from_sibling[self.at, 1 - xl]
+            away = self.buf[(1 - xl) * 2 + c] + from_sibling[self.at, 1 - xl]
+            to_across[self.at] = away.astype(BF16)
             self.second = push(to_across.at[self.at], from_across.at[self.at], across)
 
         def total(self):
             mine = self.buf[mp] + from_sibling[self.at, xl]
             self.second.wait_recv()
-            return mine + from_across[self.at]
-
-    for load in loads[:4]:
+            return mine + from_across[self.at].astype(F32)
+
+    for load in loads[:6]:
         load.wait()
     images_plane, captions_plane = PlaneGather(all_images), PlaneGather(all_captions)
-    images_plane.x1()
-    captions_plane.x1()
+    images_plane.stage("a1")
+    captions_plane.stage("a1")
 
     values = own_captions[...].reshape(ROWS, D).astype(F32)
     text_normed = layer_norm(values, text_gain[...].reshape(1, D))
-    loads[4].wait()
+    loads[6].wait()
     head_parts[mp] = dot_last(text_normed, w_head[...]).astype(BF16)
     head_copies = [
         push(head_parts.at[mp], head_parts.at[mp], peer) for peer in (sibling, across, diagonal)
     ]
 
-    images_plane.x2()
-    captions_plane.x2()
+    images_plane.stage("a2")
+    captions_plane.stage("a2")
 
     values = own_images[...].reshape(ROWS, D).astype(F32)
     normed = layer_norm(values, image_gain[...].reshape(1, D))
-    loads[5].wait()
+    for load in loads[7:10]:
+        load.wait()
     pre = dot_last(normed, w_in[...])
     act = gelu(pre, gelu_tanh(pre))
-    loads[6].wait()
+    for load in loads[10:]:
+        load.wait()
     partial[...] = dot(act, w_out[...]).reshape(partial.shape)
     feat_sum = QuadSum(partial, 0)
     feat_sum.s1()
-    images_plane.y1()
-    captions_plane.y1()
+    images_plane.stage("b1")
+    captions_plane.stage("b1")
 
     chunk = lax.broadcasted_iota(jnp.int32, (NZ, CHUNK, D), 0)
     inside = lax.broadcasted_iota(jnp.int32, (NZ, CHUNK, D), 1)
@@ -318,23 +345,19 @@
 
     feat_sum.s2()
 
-    for copy in head_copies:
-        copy.wait_recv()
-    head = jnp.concatenate([head_parts[part].astype(F32) for part in range(4)], 1)
-    head_full[...] = head.reshape(head_full.shape)
-    txt_home[...] = (head * unit_scale(head)).astype(BF16).reshape(txt_home.shape)
-    txt_units[z, 0] = txt_home[mp]
-
-    class TextRing:
+    class UnitRing:
+        def __init__(self, buf, col, share):
+            self.buf, self.col, self.sharing, self.shared = buf, col, share, []
+
         def unit(self, z_, half=None):
-            slot = txt_units.at[z_ % 8, 0]
+            slot = self.buf.at[z_ % 8, self.col]
             return slot if half is None else slot.at[pl.ds(16 * half, 16)]
 
         def share(self, z_):
-            self.shared.append(push(txt_units.at[z_ % 8, 0], txt_units.at[z_ % 8, 1], partner))
+            if self.sharing:
+                self.shared.append(push(self.unit(z_), self.buf.at[z_ % 8, 1], partner))
 
         def start(self):
-            self.shared = []
             self.up = push(self.unit(z), self.unit(z), z_up)
             self.down = push(self.unit(z), self.unit(z), z_down)
             self.share(z)
@@ -350,77 +373,70 @@
             self.down = push(unit, unit, z_down)
             self.share(z + at)
 
-        def finish(self):
+        def land(self):
             self.up.wait_recv()
             self.down.wait_recv()
             self.share(z + 4)
+
+        def finish(self):
             for copy in self.shared:
                 copy.wait_recv()
 
-    text_ring = TextRing()
-    text_ring.start()
+    for copy in head_copies:
+        copy.wait_recv()
+    head = jnp.concatenate([head_parts[part].astype(F32) for part in range(4)], 1)
+    head_full[...] = head.reshape(head_full.shape)
+    txt_home[...] = (head * unit_scale(head)).astype(BF16).reshape(txt_home.shape)
+    txt_units[z, 0] = txt_home[mp]
+
+    txt_partner = push(txt_units.at[z, 0], txt_units.at[z, 1], partner)
+    txt_rings = (UnitRing(txt_units, 0, False), UnitRing(txt_units, 1, False))
+    txt_rings[0].start()
 
     feat = own_images[mp].astype(F32) + feat_sum.total()
     feat_scale = unit_scale(feat)
     img_home[mp] = (feat * feat_scale).astype(BF16)
     img_units[z, 0] = img_home[mp]
-    img_partner = push(img_units.at[z, 0], img_units.at[z, 1], partner)
+    img_ring = UnitRing(img_units, 0, True)
+    img_ring.start()
     img_copies = [push(img_home.at[mp], img_home.at[mp], peer) for peer in (sibling, across, diagonal)]
 
-    class ImageRing:
-        def unit(self, z_, half=None):
-            return img_units.at[z_ % 8] if half is None else img_units.at[z_ % 8, half]
-
-        def start(self):
-            img_partner.wait_recv()
-            self.up = push(self.unit(z), self.unit(z), z_up)
-            self.down = push(self.unit(z), self.unit(z), z_down)
-
-        def step(self, at):
-            half = at == 3
-            self.up.wait_recv()
-            unit = self.unit(z + 8 - at, 0 if half else None)
-            self.up = push(unit, unit, z_up)
-            self.down.wait_recv()
-            unit = self.unit(z + at, 1 if half else None)
-            self.down = push(unit, unit, z_down)
-
-        def finish(self):
-            self.up.wait_recv()
-            self.down.wait_recv()
+    txt_partner.wait_recv()
+    txt_rings[1].start()
 
     def forward_block(which):
-        at = blocks[which]
-        images_plane.ready(which)
-        values = all_images[pl.ds(at * 8, 8)].reshape(256, D).astype(F32)
+        values = images_plane.block(which).astype(F32)
         normed = layer_norm(values, image_gain[...].reshape(1, D))
-        normed_t[at] = dot_last(pick_rows[...], normed).astype(BF16)
+        normed_t[which] = dot_last(pick_rows[...], normed).astype(BF16)
         pre = dot_last(normed, w_in[...])
         bend = gelu_tanh(pre)
-        act_all[at] = gelu(pre, bend)
-        slope_all[at] = gelu_slope(pre, bend)
-        captions_plane.ready(which)
-        values = all_captions[pl.ds(at * 8, 8)].reshape(256, D).astype(F32)
+        act_all[which] = gelu(pre, bend)
+        slope_all[which] = gelu_slope(pre, bend)
+        values = captions_plane.block(which).astype(F32)
         text_normed = layer_norm(values, text_gain[...].reshape(1, D))
-        text_t[at] = dot_last(pick_rows[...], text_normed).astype(BF16)
-
-    image_ring = ImageRing()
-    image_ring.start()
-    text_ring.step(1)
-    images_plane.y2()
-    captions_plane.y2()
+        text_t[which] = dot_last(pick_rows[...], text_normed).astype(BF16)
+
+    txt_rings[0].step(1)
+    txt_rings[1].step(1)
+    img_ring.step(1)
+    images_plane.stage("b2")
+    captions_plane.stage("b2")
     forward_block(0)
-    text_ring.step(2)
-    image_ring.step(1)
+    txt_rings[0].step(2)
+    txt_rings[1].step(2)
+    img_ring.step(2)
     forward_block(1)
-    text_ring.step(3)
-    image_ring.step(2)
-    images_plane.y3()
-    captions_plane.y3()
+    txt_rings[0].step(3)
+    txt_rings[1].step(3)
+    img_ring.step(3)
+    images_plane.stage("b3")
+    captions_plane.stage("b3")
     forward_block(2)
     for copy in img_copies:
         copy.wait_recv()
-    text_ring.finish()
+    img_ring.land()
+    for ring in txt_rings:
+        ring.land()
 
     img_rows = img_home[...].reshape(ROWS, D)
     units = txt_units[...].reshape(16 * QUARTER, D)
@@ -431,15 +447,7 @@
     d_img[...] = dot(slope.T.astype(BF16), units).reshape(d_img.shape)
     img_sum = QuadSum(d_img, 1)
     img_sum.s1()
-    image_ring.step(3)
-    img_sum.s2()
-    forward_block(3)
-    grad = unit_grad(feat, feat_scale, img_sum.total())
-    all_dfeat[own_slot] = grad.astype(BF16)
-    dfeat_plane = PlaneGather(all_dfeat)
-    dfeat_plane.x1()
-
-    image_ring.finish()
+    img_ring.finish()
     txt_rows = txt_home[...].reshape(ROWS, D)
     units = img_units[...].reshape(16 * QUARTER, D)
     logit = scale * dot_last(units, txt_rows) + bias
@@ -447,41 +455,45 @@
     d_txt[...] = dot(slope.T.astype(BF16), units).reshape(d_txt.shape)
     txt_sum = QuadSum(d_txt, 2)
     txt_sum.s1()
-    dfeat_plane.x2()
+    img_sum.s2()
     txt_sum.s2()
-    dfeat_plane.y1()
+    forward_block(3)
+    grad = unit_grad(feat, feat_scale, img_sum.total()).astype(BF16)
+    for half in range(2):
+        all_dfeat[half, own_slot(half)] = grad[16 * half : 16 * half + 16]
+    dfeat_plane = PlaneGather(all_dfeat)
+    dfeat_plane.stage("a1")
     head = head_full[mp]
-    grad = unit_grad(head, unit_scale(head), txt_sum.total())
-    all_dhead[own_slot] = grad.astype(BF16)
+    grad = unit_grad(head, unit_scale(head), txt_sum.total()).astype(BF16)
+    for half in range(2):
+        all_dhead[half, own_slot(half)] = grad[16 * half : 16 * half + 16]
     dhead_plane = PlaneGather(all_dhead)
-    dhead_plane.x1()
-
-    def backward_block(at):
-        d_feat = all_dfeat[pl.ds(at * 8, 8)].reshape(256, D)
-        d_pre = (dot_last(d_feat, w_out[...]) * slope_all[at]).astype(BF16)
+    dhead_plane.stage("a1")
+
+    def backward_block(which):
+        d_feat = dfeat_plane.block(which)
+        d_pre = (dot_last(d_feat, w_out[...]) * slope_all[which]).astype(BF16)
         d_feat_t = dot_last(pick_rows[...], d_feat).astype(BF16)
-        grad_in[...] += dot(normed_t[at], d_pre).reshape(grad_in.shape)
-        grad_out[...] += dot(d_feat_t, act_all[at]).reshape(grad_out.shape)
-
-    def head_block(at):
-        d_head = all_dhead[pl.ds(at * 8, 8)].reshape(256, D)
-        d_cols = dot(d_head, pick_cols[...]).astype(BF16)
-        grad = dot(text_t[at], d_cols).reshape(NZ, CHUNK, COLS)
+        grad_in[...] += dot(normed_t[which], d_pre).reshape(grad_in.shape)
+        grad_out[...] += dot(d_feat_t, act_all[which]).reshape(grad_out.shape)
+
+    def head_block(which):
+        d_cols = dot(dhead_plane.block(which), pick_cols[...]).astype(BF16)
+        grad = dot(text_t[which], d_cols).reshape(NZ, CHUNK, COLS)
         grad_head[:, pl.ds(0, CHUNK)] += grad
 
-    dfeat_plane.ready(0)
-    backward_block(blocks[0])
-    dhead_plane.x2()
-    dfeat_plane.y2()
-    dfeat_plane.ready(1)
-    backward_block(blocks[1])
-    dhead_plane.y1()
-    dfeat_plane.ready(2)
-    backward_block(blocks[2])
-    dfeat_plane.y3()
-    dhead_plane.y2()
-    dfeat_plane.ready(3)
-    backward_block(blocks[3])
+    dfeat_plane.stage("a2")
+    dhead_plane.stage("a2")
+    dfeat_plane.stage("b1")
+    dhead_plane.stage("b1")
+    backward_block(0)
+    dfeat_plane.stage("b2")
+    dhead_plane.stage("b2")
+    backward_block(1)
+    backward_block(2)
+    dfeat_plane.stage("b3")
+    dhead_plane.stage("b3")
+    backward_block(3)
 
     def pack(at):
         for part in range(3):
@@ -531,23 +543,25 @@
         ring.step(1)
     pack((z + 3) % 8)
     pack((z + 5) % 8)
+    head_block(0)
+    head_block(1)
     for ring in rings:
         ring.step(2)
+    head_block(2)
+    head_block(3)
+    ring_head.step(1)
     pack((z + 2) % 8)
     pack((z + 6) % 8)
-    dhead_plane.y3()
     for ring in rings:
         ring.step(3)
     pack((z + 1) % 8)
     pack((z + 7) % 8)
     pack(z)
+    ring_head.step(2)
     for ring in rings:
         ring.step(4)
-    for which in range(4):
-        dhead_plane.ready(which)
-        head_block(blocks[which])
-    for at in range(1, 5):
-        ring_head.step(at)
+    ring_head.step(3)
+    ring_head.step(4)
     for copy in loss_copies:
         copy.wait_recv()
     loss_out[...] = ((losses[0] + losses[1]) + (losses[2] + losses[3]))[:1]
@@ -600,16 +614,16 @@
             vmem((COLS, D), BF16),
             vmem((4, QUARTER, D), BF16),
             vmem((4, QUARTER, D), BF16),
-            vmem((32, QUARTER, D), BF16),
-            vmem((32, QUARTER, D), BF16),
-            vmem((32, QUARTER, D), BF16),
-            vmem((32, QUARTER, D), BF16),
+            vmem((2, 32, 16, D), BF16),
+            vmem((2, 32, 16, D), BF16),
+            vmem((2, 32, 16, D), BF16),
+            vmem((2, 32, 16, D), BF16),
             vmem((4, QUARTER, D), F32),
             vmem((4, QUARTER, D), F32),
             vmem((4, QUARTER, D), F32),
             vmem((3, 2, QUARTER, D), F32),
-            vmem((3, QUARTER, D), F32),
-            vmem((3, QUARTER, D), F32),
+            vmem((3, QUARTER, D), BF16),
+            vmem((3, QUARTER, D), BF16),
             vmem((4, ROWS, COLS), BF16),
             vmem((4, QUARTER, D), F32),
             vmem((4, QUARTER, D), BF16),
@@ -636,7 +650,7 @@
             vmem((2, 4, HEAD_CHUNK, COLS), BF16),
             pltpu.SemaphoreType.DMA((COPIES,)),
             pltpu.SemaphoreType.DMA((COPIES,)),
-            pltpu.SemaphoreType.DMA((7,)),
+            pltpu.SemaphoreType.DMA((13,)),
         ],
         compiler_params=pltpu.CompilerParams(
             collective_id=0, has_side_effects=True, vmem_limit_bytes=56 * 1024 * 1024

time: 118 us -> 100 us (0.85)
  Pallas kernels: 115 us -> 98.1 us
    pallas_call x1, Pallas kernels: 113 us -> 96.4 us  [on_device(): pl.pallas_call(kernel, out_shape=results, in_specs=[far, far, whole, far,...]
where the time goes in v3:
time: 100 us
  Pallas kernels  98.1 us (98%)
  between operations  1.93 us (2%)
    pallas_call x1, Pallas kernels, on_device(): pl.pallas_call(kernel, out_shape=results, in_specs=[far, far, whole, far,...  96.4 us

profile of v3, /device:TPU:32, one launch (start us, length us, event | category | flops | bytes accessed | tf_op | source)
XLA Modules:
  0.0 100.0 jit_solution(10460048213370820378)
XLA Ops:
  1.9 96.4 %window.1 = (f32[1,128]{1,0:T(1,128)}, f32[18,1076]{1,0:T(8,128)}, f32[18,1076]{1,0:T(8,128)}, f32[18,288]{1,0:T(8,128)}) custom-call(bf16[4,32,1152]{2,1,0:T(8,128)(2,1)} %bitcast.8, bf16[4,32,1152]{2,1,0:T(8,128)(2,1)} %bitcast.9, f32[1152]{0:T(1024)} %image_gain.1, bf16[1076,1152]{1,0:T(8,128)(2,1)} %bitcast.6, bf16[1076,1152]{1,0:T(8,128)(2,1)} %fc_out.1, ...), custom_call_target="tpu_custom_call" | custom-call | tf_op jit(solution)/shard_map/window/pallas_call | solution.py:606
  98.4 1.7 %results.1 = (f32[1,128]{1,0:T(1,128)}, f32[18,1076]{1,0:T(8,128)}, f32[18,1076]{1,0:T(8,128)}, f32[18,288]{1,0:T(8,128)}) custom-call(f32[1,128]{1,0:T(1,128)} %get-tuple-element.12.refs_0_, f32[18,1076]{1,0:T(8,128)} %get-tuple-element.13.refs_1_, f32[18,1076]{1,0:T(8,128)} %get-tuple-element.14.refs_2_, f32[18,288]{1,0:T(8,128)} %get-tuple-element.15.refs_3_), custom_call_target="tpu_custom_call" | custom-call | tf_op jit(solution)/shard_map/results/pallas_call | solution.py:671

commit v4 on v3

--- a/solution.py
+++ b/solution.py
@@ -135,7 +135,6 @@
     act_all,
     slope_all,
     normed_t,
-    text_t,
     grad_in,
     grad_out,
     grad_head,
@@ -191,14 +190,14 @@
         load.start()
 
     barrier = pltpu.get_barrier_semaphore()
-    peers = (sibling, across, diagonal, partner, y_up, y_down, z_up, z_down)
+    rounds = [place((z + step) % 8, xh, y, xl, c) for step in range(1, NZ)]
+    peers = [sibling, across, diagonal, partner, y_up, y_down] + rounds
     for peer in peers:
         pl.semaphore_signal(barrier, inc=1, device_id=peer, device_id_type=pl.DeviceIdType.MESH)
 
     scale, bias = logit_scale[0], logit_bias[0]
     links = Links(send_sems, recv_sems)
     push = links.push
-    pl.semaphore_wait(barrier, len(peers))
 
     class HalfGather:
         def __init__(self, buf, half, lead, follow):
@@ -289,22 +288,20 @@
             self.second.wait_recv()
             return mine + from_across[self.at].astype(F32)
 
+    images_plane, captions_plane = PlaneGather(all_images), PlaneGather(all_captions)
     for load in loads[:6]:
         load.wait()
-    images_plane, captions_plane = PlaneGather(all_images), PlaneGather(all_captions)
-    images_plane.stage("a1")
-    captions_plane.stage("a1")
 
     values = own_captions[...].reshape(ROWS, D).astype(F32)
     text_normed = layer_norm(values, text_gain[...].reshape(1, D))
     loads[6].wait()
     head_parts[mp] = dot_last(text_normed, w_head[...]).astype(BF16)
+    pl.semaphore_wait(barrier, len(peers))
+    images_plane.stage("a1")
+    captions_plane.stage("a1")
     head_copies = [
         push(head_parts.at[mp], head_parts.at[mp], peer) for peer in (sibling, across, diagonal)
     ]
-
-    images_plane.stage("a2")
-    captions_plane.stage("a2")
 
     values = own_images[...].reshape(ROWS, D).astype(F32)
     normed = layer_norm(values, image_gain[...].reshape(1, D))
@@ -317,8 +314,8 @@
     partial[...] = dot(act, w_out[...]).reshape(partial.shape)
     feat_sum = QuadSum(partial, 0)
     feat_sum.s1()
-    images_plane.stage("b1")
-    captions_plane.stage("b1")
+    images_plane.stage("a2")
+    captions_plane.stage("a2")
 
     chunk = lax.broadcasted_iota(jnp.int32, (NZ, CHUNK, D), 0)
     inside = lax.broadcasted_iota(jnp.int32, (NZ, CHUNK, D), 1)
@@ -392,6 +389,8 @@
     txt_partner = push(txt_units.at[z, 0], txt_units.at[z, 1], partner)
     txt_rings = (UnitRing(txt_units, 0, False), UnitRing(txt_units, 1, False))
     txt_rings[0].start()
+    images_plane.stage("b1")
+    captions_plane.stage("b1")
 
     feat = own_images[mp].astype(F32) + feat_sum.total()
     feat_scale = unit_scale(feat)
@@ -412,31 +411,28 @@
         bend = gelu_tanh(pre)
         act_all[which] = gelu(pre, bend)
         slope_all[which] = gelu_slope(pre, bend)
-        values = captions_plane.block(which).astype(F32)
-        text_normed = layer_norm(values, text_gain[...].reshape(1, D))
-        text_t[which] = dot_last(pick_rows[...], text_normed).astype(BF16)
 
     txt_rings[0].step(1)
     txt_rings[1].step(1)
     img_ring.step(1)
     images_plane.stage("b2")
-    captions_plane.stage("b2")
-    forward_block(0)
     txt_rings[0].step(2)
     txt_rings[1].step(2)
     img_ring.step(2)
-    forward_block(1)
+    captions_plane.stage("b2")
+    forward_block(0)
     txt_rings[0].step(3)
     txt_rings[1].step(3)
     img_ring.step(3)
     images_plane.stage("b3")
-    captions_plane.stage("b3")
-    forward_block(2)
+    forward_block(1)
     for copy in img_copies:
         copy.wait_recv()
     img_ring.land()
     for ring in txt_rings:
         ring.land()
+
+    captions_plane.stage("b3")
 
     img_rows = img_home[...].reshape(ROWS, D)
     units = txt_units[...].reshape(16 * QUARTER, D)
@@ -447,6 +443,8 @@
     d_img[...] = dot(slope.T.astype(BF16), units).reshape(d_img.shape)
     img_sum = QuadSum(d_img, 1)
     img_sum.s1()
+    img_sum.s2()
+    forward_block(2)
     img_ring.finish()
     txt_rows = txt_home[...].reshape(ROWS, D)
     units = img_units[...].reshape(16 * QUARTER, D)
@@ -455,14 +453,13 @@
     d_txt[...] = dot(slope.T.astype(BF16), units).reshape(d_txt.shape)
     txt_sum = QuadSum(d_txt, 2)
     txt_sum.s1()
-    img_sum.s2()
-    txt_sum.s2()
-    forward_block(3)
     grad = unit_grad(feat, feat_scale, img_sum.total()).astype(BF16)
     for half in range(2):
         all_dfeat[half, own_slot(half)] = grad[16 * half : 16 * half + 16]
     dfeat_plane = PlaneGather(all_dfeat)
     dfeat_plane.stage("a1")
+    txt_sum.s2()
+    forward_block(3)
     head = head_full[mp]
     grad = unit_grad(head, unit_scale(head), txt_sum.total()).astype(BF16)
     for half in range(2):
@@ -478,8 +475,11 @@
         grad_out[...] += dot(d_feat_t, act_all[which]).reshape(grad_out.shape)
 
     def head_block(which):
+        values = captions_plane.block(which).astype(F32)
+        text_normed = layer_norm(values, text_gain[...].reshape(1, D))
+        text_t = dot_last(pick_rows[...], text_normed).astype(BF16)
         d_cols = dot(dhead_plane.block(which), pick_cols[...]).astype(BF16)
-        grad = dot(text_t[which], d_cols).reshape(NZ, CHUNK, COLS)
+        grad = dot(text_t, d_cols).reshape(NZ, CHUNK, COLS)
         grad_head[:, pl.ds(0, CHUNK)] += grad
 
     dfeat_plane.stage("a2")
@@ -537,7 +537,6 @@
         RingSum(packed, first, stage_main, land_main, True),
         RingSum(packed, second, stage_main, land_main, False),
     )
-    ring_head = RingSum(grad_head, pl.ds(0, HEAD_CHUNK), stage_head, land_head, True)
     pack((z + 4) % 8)
     for ring in rings:
         ring.step(1)
@@ -549,7 +548,11 @@
         ring.step(2)
     head_block(2)
     head_block(3)
-    ring_head.step(1)
+    head_sends = []
+    for step in range(1, NZ):
+        stage_head[step - 1] = grad_head[(z + step) % 8].astype(BF16)
+        slot = (stage_head.at[step - 1], land_head.at[step - 1])
+        head_sends.append(push(*slot, rounds[step - 1]))
     pack((z + 2) % 8)
     pack((z + 6) % 8)
     for ring in rings:
@@ -557,11 +560,8 @@
     pack((z + 1) % 8)
     pack((z + 7) % 8)
     pack(z)
-    ring_head.step(2)
     for ring in rings:
         ring.step(4)
-    ring_head.step(3)
-    ring_head.step(4)
     for copy in loss_copies:
         copy.wait_recv()
     loss_out[...] = ((losses[0] + losses[1]) + (losses[2] + losses[3]))[:1]
@@ -572,7 +572,11 @@
         lanes = pl.ds(384 * part, width)
         in_out[:, lanes] = packed[z, pl.ds(OUT * part, OUT), pl.ds(0, width)]
         out_out[:, lanes] = packed[z, pl.ds(OUT * (part + 3), OUT), pl.ds(0, width)]
-    head_out[...] = ring_head.total()[:OUT]
+    total = grad_head[z]
+    for step in range(1, NZ):
+        head_sends[step - 1].wait_recv()
+        total += land_head[step - 1].astype(F32)
+    head_out[...] = total[:OUT]
     links.drain()
 
 
@@ -639,15 +643,14 @@
             vmem((4, 256, HIDDEN), BF16),
             vmem((4, 256, HIDDEN), F32),
             vmem((4, NZ * CHUNK, 256), BF16),
-            vmem((4, NZ * CHUNK, 256), BF16),
             vmem((NZ, CHUNK, HIDDEN), F32),
             vmem((NZ, CHUNK, HIDDEN), F32),
             vmem((NZ, HEAD_CHUNK, COLS), F32),
             vmem((NZ, 112, 384), F32),
             vmem((2, 4, 112, 384), BF16),
-            vmem((2, 4, HEAD_CHUNK, COLS), BF16),
+            vmem((NZ - 1, HEAD_CHUNK, COLS), BF16),
             vmem((2, 4, 112, 384), BF16),
-            vmem((2, 4, HEAD_CHUNK, COLS), BF16),
+            vmem((NZ - 1, HEAD_CHUNK, COLS), BF16),
             pltpu.SemaphoreType.DMA((COPIES,)),
             pltpu.SemaphoreType.DMA((COPIES,)),
             pltpu.SemaphoreType.DMA((13,)),

time: 100 us -> 95.6 us (0.956)
  Pallas kernels: 98.1 us -> 92.9 us
    pallas_call x1, Pallas kernels: 96.4 us -> 91.3 us  [on_device(): pl.pallas_call(kernel, out_shape=results, in_specs=[far, far, whole, far,...]
where the time goes in v4:
time: 95.6 us; the launch traced here: 94.9 us
  Pallas kernels  92.9 us (97%)
  between operations  1.93 us (2%)
    pallas_call x1, Pallas kernels, on_device(): pl.pallas_call(kernel, out_shape=results, in_specs=[far, far, whole, far,...  91.3 us

profile of v4, /device:TPU:32, one launch (start us, length us, event | category | flops | bytes accessed | tf_op | source)
XLA Modules:
  0.0 94.9 jit_solution(16377647951790813931)
XLA Ops:
  1.9 91.3 %window.1 = (f32[1,128]{1,0:T(1,128)}, f32[18,1076]{1,0:T(8,128)}, f32[18,1076]{1,0:T(8,128)}, f32[18,288]{1,0:T(8,128)}) custom-call(bf16[4,32,1152]{2,1,0:T(8,128)(2,1)} %bitcast.8, bf16[4,32,1152]{2,1,0:T(8,128)(2,1)} %bitcast.9, f32[1152]{0:T(1024)} %image_gain.1, bf16[1076,1152]{1,0:T(8,128)(2,1)} %bitcast.6, bf16[1076,1152]{1,0:T(8,128)(2,1)} %fc_out.1, ...), custom_call_target="tpu_custom_call" | custom-call | tf_op jit(solution)/shard_map/window/pallas_call | solution.py:610
  93.2 1.7 %results.1 = (f32[1,128]{1,0:T(1,128)}, f32[18,1076]{1,0:T(8,128)}, f32[18,1076]{1,0:T(8,128)}, f32[18,288]{1,0:T(8,128)}) custom-call(f32[1,128]{1,0:T(1,128)} %get-tuple-element.12.refs_0_, f32[18,1076]{1,0:T(8,128)} %get-tuple-element.13.refs_1_, f32[18,1076]{1,0:T(8,128)} %get-tuple-element.14.refs_2_, f32[18,288]{1,0:T(8,128)} %get-tuple-element.15.refs_3_), custom_call_target="tpu_custom_call" | custom-call | tf_op jit(solution)/shard_map/results/pallas_call | solution.py:674

commit v5 on v4

--- a/solution.py
+++ b/solution.py
@@ -135,6 +135,7 @@
     act_all,
     slope_all,
     normed_t,
+    text_t,
     grad_in,
     grad_out,
     grad_head,
@@ -460,6 +461,7 @@
     dfeat_plane.stage("a1")
     txt_sum.s2()
     forward_block(3)
+    dfeat_plane.stage("a2")
     head = head_full[mp]
     grad = unit_grad(head, unit_scale(head), txt_sum.total()).astype(BF16)
     for half in range(2):
@@ -474,25 +476,29 @@
         grad_in[...] += dot(normed_t[which], d_pre).reshape(grad_in.shape)
         grad_out[...] += dot(d_feat_t, act_all[which]).reshape(grad_out.shape)
 
-    def head_block(which):
+    def text_block(which):
         values = captions_plane.block(which).astype(F32)
         text_normed = layer_norm(values, text_gain[...].reshape(1, D))
-        text_t = dot_last(pick_rows[...], text_normed).astype(BF16)
+        text_t[which] = dot_last(pick_rows[...], text_normed).astype(BF16)
+
+    def head_block(which):
         d_cols = dot(dhead_plane.block(which), pick_cols[...]).astype(BF16)
-        grad = dot(text_t, d_cols).reshape(NZ, CHUNK, COLS)
+        grad = dot(text_t[which], d_cols).reshape(NZ, CHUNK, COLS)
         grad_head[:, pl.ds(0, CHUNK)] += grad
 
-    dfeat_plane.stage("a2")
+    dfeat_plane.stage("b1")
     dhead_plane.stage("a2")
-    dfeat_plane.stage("b1")
+    text_block(0)
+    text_block(1)
+    backward_block(0)
     dhead_plane.stage("b1")
-    backward_block(0)
+    text_block(2)
+    text_block(3)
     dfeat_plane.stage("b2")
-    dhead_plane.stage("b2")
     backward_block(1)
     backward_block(2)
+    dhead_plane.stage("b2")
     dfeat_plane.stage("b3")
-    dhead_plane.stage("b3")
     backward_block(3)
 
     def pack(at):
@@ -540,6 +546,7 @@
     pack((z + 4) % 8)
     for ring in rings:
         ring.step(1)
+    dhead_plane.stage("b3")
     pack((z + 3) % 8)
     pack((z + 5) % 8)
     head_block(0)
@@ -643,6 +650,7 @@
             vmem((4, 256, HIDDEN), BF16),
             vmem((4, 256, HIDDEN), F32),
             vmem((4, NZ * CHUNK, 256), BF16),
+            vmem((4, NZ * CHUNK, 256), BF16),
             vmem((NZ, CHUNK, HIDDEN), F32),
             vmem((NZ, CHUNK, HIDDEN), F32),
             vmem((NZ, HEAD_CHUNK, COLS), F32),

time: 95.6 us -> 91.6 us (0.958)
  Pallas kernels: 92.9 us -> 89.5 us
    pallas_call x1, Pallas kernels: 91.3 us -> 87.9 us  [on_device(): pl.pallas_call(kernel, out_shape=results, in_specs=[far, far, whole, far,...]
where the time goes in v5:
time: 91.6 us; the launch traced here: 91.5 us
  Pallas kernels  89.5 us (98%)
  between operations  1.93 us (2%)
    pallas_call x1, Pallas kernels, on_device(): pl.pallas_call(kernel, out_shape=results, in_specs=[far, far, whole, far,...  87.9 us

profile of v5, /device:TPU:32, one launch (start us, length us, event | category | flops | bytes accessed | tf_op | source)
XLA Modules:
  0.0 91.5 jit_solution(17770140597946187849)
XLA Ops:
  1.9 87.9 %window.1 = (f32[1,128]{1,0:T(1,128)}, f32[18,1076]{1,0:T(8,128)}, f32[18,1076]{1,0:T(8,128)}, f32[18,288]{1,0:T(8,128)}) custom-call(bf16[4,32,1152]{2,1,0:T(8,128)(2,1)} %bitcast.8, bf16[4,32,1152]{2,1,0:T(8,128)(2,1)} %bitcast.9, f32[1152]{0:T(1024)} %image_gain.1, bf16[1076,1152]{1,0:T(8,128)(2,1)} %bitcast.6, bf16[1076,1152]{1,0:T(8,128)(2,1)} %fc_out.1, ...), custom_call_target="tpu_custom_call" | custom-call | tf_op jit(solution)/shard_map/window/pallas_call | solution.py:617
  89.8 1.7 %results.1 = (f32[1,128]{1,0:T(1,128)}, f32[18,1076]{1,0:T(8,128)}, f32[18,1076]{1,0:T(8,128)}, f32[18,288]{1,0:T(8,128)}) custom-call(f32[1,128]{1,0:T(1,128)} %get-tuple-element.12.refs_0_, f32[18,1076]{1,0:T(8,128)} %get-tuple-element.13.refs_1_, f32[18,1076]{1,0:T(8,128)} %get-tuple-element.14.refs_2_, f32[18,288]{1,0:T(8,128)} %get-tuple-element.15.refs_3_), custom_call_target="tpu_custom_call" | custom-call | tf_op jit(solution)/shard_map/results/pallas_call | solution.py:682

commit v6 on v5

--- a/solution.py
+++ b/solution.py
@@ -420,20 +420,17 @@
     txt_rings[0].step(2)
     txt_rings[1].step(2)
     img_ring.step(2)
-    captions_plane.stage("b2")
-    forward_block(0)
     txt_rings[0].step(3)
     txt_rings[1].step(3)
     img_ring.step(3)
     images_plane.stage("b3")
+    forward_block(0)
     forward_block(1)
     for copy in img_copies:
         copy.wait_recv()
     img_ring.land()
     for ring in txt_rings:
         ring.land()
-
-    captions_plane.stage("b3")
 
     img_rows = img_home[...].reshape(ROWS, D)
     units = txt_units[...].reshape(16 * QUARTER, D)
@@ -445,6 +442,7 @@
     img_sum = QuadSum(d_img, 1)
     img_sum.s1()
     img_sum.s2()
+    captions_plane.stage("b2")
     forward_block(2)
     img_ring.finish()
     txt_rows = txt_home[...].reshape(ROWS, D)
@@ -460,6 +458,7 @@
     dfeat_plane = PlaneGather(all_dfeat)
     dfeat_plane.stage("a1")
     txt_sum.s2()
+    captions_plane.stage("b3")
     forward_block(3)
     dfeat_plane.stage("a2")
     head = head_full[mp]

time: 91.6 us -> 92.1 us (level)
  no operation moved by 1% of the time
where the time goes in v6:
time: 92.1 us; the launch traced here: 92 us
  Pallas kernels  90.1 us (98%)
  between operations  1.93 us (2%)
    pallas_call x1, Pallas kernels, on_device(): pl.pallas_call(kernel, out_shape=results, in_specs=[far, far, whole, far,...  88.4 us

profile of v6, /device:TPU:32, one launch (start us, length us, event | category | flops | bytes accessed | tf_op | source)
XLA Modules:
  0.0 92.0 jit_solution(12371278015219623727)
XLA Ops:
  1.9 88.4 %window.1 = (f32[1,128]{1,0:T(1,128)}, f32[18,1076]{1,0:T(8,128)}, f32[18,1076]{1,0:T(8,128)}, f32[18,288]{1,0:T(8,128)}) custom-call(bf16[4,32,1152]{2,1,0:T(8,128)(2,1)} %bitcast.8, bf16[4,32,1152]{2,1,0:T(8,128)(2,1)} %bitcast.9, f32[1152]{0:T(1024)} %image_gain.1, bf16[1076,1152]{1,0:T(8,128)(2,1)} %bitcast.6, bf16[1076,1152]{1,0:T(8,128)(2,1)} %fc_out.1, ...), custom_call_target="tpu_custom_call" | custom-call | tf_op jit(solution)/shard_map/window/pallas_call | solution.py:616
  90.3 1.7 %results.1 = (f32[1,128]{1,0:T(1,128)}, f32[18,1076]{1,0:T(8,128)}, f32[18,1076]{1,0:T(8,128)}, f32[18,288]{1,0:T(8,128)}) custom-call(f32[1,128]{1,0:T(1,128)} %get-tuple-element.12.refs_0_, f32[18,1076]{1,0:T(8,128)} %get-tuple-element.13.refs_1_, f32[18,1076]{1,0:T(8,128)} %get-tuple-element.14.refs_2_, f32[18,288]{1,0:T(8,128)} %get-tuple-element.15.refs_3_), custom_call_target="tpu_custom_call" | custom-call | tf_op jit(solution)/shard_map/results/pallas_call | solution.py:681
